TPU v7x, 256 devices: a whole 4x4x8 slice. The times are simulated.
256 devices in a mesh: seq: 64 (over z, x_lo, y), ch: 4 (over x_hi, core).
Axes of the slice: x: 4 (x_hi: 2, x_lo: 2; x = x_hi * 2 + x_lo), y: 4, z: 8, core: 2. Of those that a mesh axis runs over, the one named last changes fastest.
Arguments:
- tokens: bfloat16 [8192, 2048], P('seq'), may hold values from -16 to 16
- value_weight: bfloat16 [2048, 2048], P(None, 'ch'), may hold values from -0.125 to 0.125
- gate_weight: bfloat16 [2048, 2048], P(None, 'ch'), may hold values from -0.125 to 0.125
- filters: float32 [8192, 2048], P('seq', 'ch'), may hold values from -0.0625 to 0.0625
- cotangent: bfloat16 [8192, 2048], P('seq', 'ch'), may hold values from -6 to 6
Outputs:
- input_grad: bfloat16 [8192, 2048], P('seq', 'ch')
- filter_grad: float32 [8192, 2048], P('seq', 'ch')
- value_weight_grad: float32 [2048, 2048], P('seq', 'ch')
- gate_weight_grad: float32 [2048, 2048], P('seq', 'ch')
All inputs are finite; a program needn't handle non-finite values.
Results may differ from a plain program's by a relative error of at most 0.0049.
Values may be sent and summed in bfloat16 or wider, within the bound.
A program may use at most 128 MiB of HBM per device.

v0:
```python
import math

import jax
import jax.numpy as jnp
from jax import lax
from jax.sharding import PartitionSpec as P


def angles(first, second, modulus):
    phase = first[:, None] * second[None, :] % modulus
    return phase.astype(jnp.float32) * (2.0 * math.pi / modulus)


def rows_apply(table, field):
    return jnp.einsum("br,fxrc->fxbc", table, field, precision=lax.Precision.HIGHEST)


def blocks_apply(table, field):
    return jnp.einsum("ap,fprc->farc", table, field, precision=lax.Precision.HIGHEST)


def local(tokens, value_weight, gate_weight, filters, cotangent):
    tok_rows, model_width = tokens.shape
    channels = value_weight.shape[1]
    seq_count = lax.axis_size("seq")
    seq_index = lax.axis_index("seq")
    padded = 2 * tok_rows * seq_count
    piece_rows = tok_rows // seq_count
    grad_scale = (tok_rows * seq_count) ** (-0.5)
    tok_full = tokens.astype(jnp.float32)
    values = jnp.dot(tok_full, value_weight.astype(jnp.float32), preferred_element_type=jnp.float32)
    gating = jnp.dot(tok_full, gate_weight.astype(jnp.float32), preferred_element_type=jnp.float32)
    cot_full = cotangent.astype(jnp.float32)
    upstream = cot_full * gating
    signals = jnp.stack([values, filters, upstream])[:, None]
    columns = lax.all_to_all(signals, "seq", split_axis=2, concat_axis=1, tiled=True)
    blocks = jnp.arange(seq_count, dtype=jnp.int32)
    freq_low = jnp.arange(2 * seq_count, dtype=jnp.int32)
    block_ang = angles(freq_low, blocks, 2 * seq_count)
    block_cos = jnp.cos(block_ang)
    block_sin = jnp.sin(block_ang)
    low_real = blocks_apply(block_cos, columns)
    low_imag = -blocks_apply(block_sin, columns)
    local_rows = seq_index * piece_rows + jnp.arange(piece_rows, dtype=jnp.int32)
    twist_ang = angles(freq_low, local_rows, padded)[None, :, :, None]
    twist_cos = jnp.cos(twist_ang)
    twist_sin = jnp.sin(twist_ang)
    turned_real = low_real * twist_cos + low_imag * twist_sin
    turned_imag = low_imag * twist_cos - low_real * twist_sin
    owned = lax.all_to_all(
        jnp.concatenate([turned_real, turned_imag]), "seq", split_axis=1, concat_axis=2, tiled=True
    )
    own_real = owned[:3]
    own_imag = owned[3:]
    all_rows = jnp.arange(tok_rows, dtype=jnp.int32)
    row_ang = angles(all_rows, all_rows, tok_rows)
    row_cos = jnp.cos(row_ang)
    row_sin = jnp.sin(row_ang)
    spec_real = rows_apply(row_cos, own_real) + rows_apply(row_sin, own_imag)
    spec_imag = rows_apply(row_cos, own_imag) - rows_apply(row_sin, own_real)
    val_re, fil_re, up_re = (spec_real[0], spec_real[1], spec_real[2])
    val_im, fil_im, up_im = (spec_imag[0], spec_imag[1], spec_imag[2])
    prod_real = jnp.stack(
        [
            val_re * fil_re - val_im * fil_im,
            fil_re * up_re + fil_im * up_im,
            val_re * up_re + val_im * up_im,
        ]
    )
    prod_imag = jnp.stack(
        [
            val_re * fil_im + val_im * fil_re,
            fil_re * up_im - fil_im * up_re,
            val_re * up_im - val_im * up_re,
        ]
    )
    inv_real = rows_apply(row_cos, prod_real) - rows_apply(row_sin, prod_imag)
    inv_imag = rows_apply(row_cos, prod_imag) + rows_apply(row_sin, prod_real)
    owned_freq = 2 * seq_index + jnp.arange(2, dtype=jnp.int32)
    wind_ang = angles(owned_freq, all_rows, padded)[None, :, :, None]
    wind_cos = jnp.cos(wind_ang)
    wind_sin = jnp.sin(wind_ang)
    wound_real = inv_real * wind_cos - inv_imag * wind_sin
    wound_imag = inv_imag * wind_cos + inv_real * wind_sin
    gathered = lax.all_to_all(
        jnp.concatenate([wound_real, wound_imag]), "seq", split_axis=2, concat_axis=1, tiled=True
    )
    outer_ang = angles(blocks, freq_low, 2 * seq_count)
    outer_cos = jnp.cos(outer_ang)
    outer_sin = jnp.sin(outer_ang)
    fields = (
        blocks_apply(outer_cos, gathered[:3]) - blocks_apply(outer_sin, gathered[3:])
    ) / padded
    result = lax.all_to_all(fields, "seq", split_axis=1, concat_axis=2, tiled=True)[:, 0]
    conv_out = result[0]
    value_grad = result[1].astype(jnp.bfloat16)
    filter_grad = result[2] * grad_scale
    gate_grad = (cot_full * conv_out).astype(jnp.bfloat16)
    stacked_grads = jnp.concatenate([value_grad, gate_grad], axis=1).astype(jnp.float32)
    summed = (
        lax.psum_scatter(
            jnp.dot(tok_full.T, stacked_grads, preferred_element_type=jnp.float32),
            "seq",
            scatter_dimension=0,
            tiled=True,
        )
        * grad_scale
    )
    value_weight_grad = summed[:, :channels]
    gate_weight_grad = summed[:, channels:]
    partial_sum = jnp.dot(
        value_grad.astype(jnp.float32),
        value_weight.astype(jnp.float32).T,
        preferred_element_type=jnp.float32,
    ) + jnp.dot(
        gate_grad.astype(jnp.float32),
        gate_weight.astype(jnp.float32).T,
        preferred_element_type=jnp.float32,
    )
    input_grad = lax.psum_scatter(partial_sum, "ch", scatter_dimension=1, tiled=True).astype(
        jnp.bfloat16
    )
    return (input_grad, filter_grad, value_weight_grad, gate_weight_grad)


def solution(mesh):
    placed = (P("seq", None), P(None, "ch"), P(None, "ch"), P("seq", "ch"), P("seq", "ch"))
    return jax.shard_map(
        local,
        mesh=mesh,
        in_specs=placed,
        out_specs=(P("seq", "ch"), P("seq", "ch"), P("seq", "ch"), P("seq", "ch")),
        check_vma=False,
    )
```

profile of v0, /device:TPU:4, one launch (start us, length us, event | category | flops | bytes accessed | tf_op | source)
XLA Modules:
  0.0 696.5 jit_solution(9500573401433955339)
XLA Ops:
  13.0 12.7 %all-to-all-start = ((f32[3,1,128,512]{3,1,0,2:T(1,128)}), f32[3,1,128,512]{3,1,0,2:T(1,128)S(1)}, u32[]{:S(2)}, u32[]{:S(2)}) async-start(f32[3,1,128,512]{3,1,0,2:T(1,128)} %copy.71), calls=%async_computation | async-start | bytes 1572864 | tf_op jit(solution)/shard_map/all_to_all | solution.py:36
  25.9 22.9 %all-to-all-done = f32[3,1,128,512]{3,1,0,2:T(1,128)S(1)} async-done(((f32[3,1,128,512]{3,1,0,2:T(1,128)}), f32[3,1,128,512]{3,1,0,2:T(1,128)S(1)}, u32[]{:S(2)}, u32[]{:S(2)}) %all-to-all-start) | async-done | bytes 786464 | tf_op jit(solution)/shard_map/all_to_all | solution.py:36
  49.0 2.9 fusion.8
  51.9 3.0 fusion
  54.9 1.9 pad_maximum_fusion
  56.8 5.8 copy.75
  62.7 6.4 all-to-all-start.1
  69.1 12.7 %reduce-scatter.5.cloned.1.call-start = ((), (), s32[]{:S(2)}) async-start(), calls=%async_computation.6 | async-start | bytes 1310720 | tf_op jit(solution)/shard_map/reduce_scatter | solution.py:120
  81.9 58.1 %all-to-all-done.1 = f32[6,128,2,512]{3,2,0,1:T(2,128)} async-done(((f32[6,128,2,512]{3,2,0,1:T(2,128)}), f32[6,128,2,512]{3,2,0,1:T(2,128)}, u32[]{:S(2)}, u32[]{:S(2)}) %all-to-all-start.1) | async-done | bytes 3145760 | tf_op jit(solution)/shard_map/all_to_all | solution.py:50
  140.0 3.0 copy.76
  143.0 2.5 fusion.129
  145.5 1.9 copy.77
  147.4 3.7 copy.78
  151.1 4.3 fusion.25
  155.4 2.0 copy.79
  157.4 3.7 copy.80
  161.0 3.2 fusion.23
  173.2 2.1 subtract_bitcast_fusion
  175.3 1.8 pad_maximum_fusion.1
  177.2 5.9 copy.83
  183.1 79.6 %all_to_all.51 = f32[6,2,128,512]{3,1,0,2:T(2,128)S(1)} all-to-all(f32[6,2,128,512]{3,1,0,2:T(2,128)} %copy.83), channel_id=1, replica_groups=mesh['seq'=64,'ch'=4] {'seq'}, dimensions={2} | all-to-all | bytes 6291456 | tf_op jit(solution)/shard_map/all_to_all | solution.py:85
  263.7 2.5 fusion.128
  267.9 3.2 slice.75
  271.1 3.1 copy.85
  274.2 3.1 slice.73
  277.3 2.7 fusion.37
  281.8 28.0 %all_to_all.52 = f32[3,64,2,512]{3,2,0,1:T(2,128)S(1)} all-to-all(f32[3,64,2,512]{3,2,0,1:T(2,128)S(1)} %copy.87), channel_id=1, replica_groups=mesh['seq'=64,'ch'=4] {'seq'}, dimensions={1} | all-to-all | bytes 1572864 | tf_op jit(solution)/shard_map/all_to_all | solution.py:94
  316.3 1.8 convolution_add_fusion
  318.2 4.5 convolution_bitcast_fusion
  322.7 9.4 %copy.96 = f32[2048,1024]{1,0:T(8,128)} copy(f32[2048,1024]{0,1:T(8,128)} %convolution_bitcast_fusion) | data formatting | bytes 16777216
  333.9 15.4 %reduce-scatter.5.cloned.1.call-done = f32[128,512]{1,0:T(8,128)} async-done(((f32[128,2048]{1,0:T(8,128)}), f32[128,512]{1,0:T(8,128)}) %reduce-scatter.5.cloned.1.call-update) | async-done | bytes 262160 | tf_op jit(solution)/shard_map/reduce_scatter | solution.py:120
  350.9 335.6 %reduce-scatter.7.cloned.1.call-done = f32[32,1024]{1,0:T(8,128)} async-done(((f32[2048,1024]{1,0:T(8,128)}), f32[32,1024]{1,0:T(8,128)}) %reduce-scatter.7.cloned.1.call-update) | async-done | bytes 131088
  (59 shorter events, 32.2 us)
Async XLA Ops:
  7.2 1.6 copy-start
  7.2 3.1 copy-start.8
  7.2 3.1 copy-start.10
  7.2 3.1 copy-start.3
  10.3 1.0 copy-start.11
  13.0 35.7 %all-to-all-start = ((f32[3,1,128,512]{3,1,0,2:T(1,128)}), f32[3,1,128,512]{3,1,0,2:T(1,128)S(1)}, u32[]{:S(2)}, u32[]{:S(2)}) async-start(f32[3,1,128,512]{3,1,0,2:T(1,128)} %copy.71), calls=%async_computation | async-start | bytes 1572864 | tf_op jit(solution)/shard_map/all_to_all | solution.py:36
  62.7 77.3 %all-to-all-start.1 = ((f32[6,128,2,512]{3,2,0,1:T(2,128)}), f32[6,128,2,512]{3,2,0,1:T(2,128)}, u32[]{:S(2)}, u32[]{:S(2)}) async-start(f32[6,128,2,512]{3,2,0,1:T(2,128)} %copy.75), calls=%async_computation.1 | async-start | bytes 6291456 | tf_op jit(solution)/shard_map/all_to_all | solution.py:50
  69.1 280.2 %reduce-scatter.5.cloned.1.call-start = ((), (), s32[]{:S(2)}) async-start(), calls=%async_computation.6 | async-start | bytes 1310720 | tf_op jit(solution)/shard_map/reduce_scatter | solution.py:120
  151.1 4.3 copy-start.6
  161.0 3.2 copy-start.2
  161.0 3.2 copy-start.7
  164.3 1.7 copy-start.1
  277.3 2.7 copy-start.5
  314.7 1.6 copy-start.4
  318.1 368.4 %reduce-scatter.7.cloned.1.call-start = ((), (), s32[]{:S(2)}) async-start(), calls=%async_computation.7 | async-start | bytes 8519680
  332.1 0.9 copy-start.9
Sparse Core Ops, SparseCore 0:
  318.2 31.0 reduce-scatter.4
  352.0 334.4 reduce-scatter.6
where the time goes:
time: 705 us; the launch traced here: 696 us
  waiting for transfers between devices  432 us (61%)
  blocking collectives  108 us (15%)
  local copies, waits for them, and re-layouts  65.2 us (9%)
  matrix products  37 us (5%)
  starting transfers between devices  31.8 us (5%)
  between operations  14.8 us (2%)
  other arithmetic  8.02 us (1%)
    unnamed x3, waiting for transfers between devices  336 us
    all_to_all x1, blocking collectives, local(): lax.all_to_all(jnp.concatenate([wound_real, wound_imag]), 'seq', split_ax...  79.6 us
    all_to_all x1, waiting for transfers between devices, local(): lax.all_to_all(jnp.concatenate([turned_real, turned_imag]), 'seq', split_...  58.1 us
    all_to_all x1, blocking collectives, local(): lax.all_to_all(fields, 'seq', split_axis=1, concat_axis=2, tiled=True)[:, 0]  28 us
    all_to_all x1, waiting for transfers between devices, local(): lax.all_to_all(signals, 'seq', split_axis=2, concat_axis=1, tiled=True)  22.9 us
    dot_general x8, matrix products, rows_apply(): jnp.einsum('br,fxrc->fxbc', table, field, precision=lax.Precision.HIGHEST)  18.1 us
    unnamed x29, local copies, waits for them, and re-layouts  16 us
    reduce_scatter x1, waiting for transfers between devices, local(): lax.psum_scatter(partial_sum, 'ch', scatter_dimension=1, tiled=True)  15.4 us
  transfers between devices with their start and end apart: 4, of which 4 were waited for; matrix products, arithmetic and copies ran while one was open for 2% of the time, Pallas kernels for 0%

commit v1 on v0

v1 whole, which is shorter than its diff:
```python
import functools
import math

import jax
import jax.numpy as jnp
import ml_dtypes
import numpy as np
from jax import lax
from jax.experimental import pallas as pl
from jax.experimental.pallas import tpu as pltpu
from jax.sharding import PartitionSpec as P

MESH = pl.DeviceIdType.MESH
F32 = jnp.float32
BF16 = jnp.bfloat16
SIDE = 128
PADDED = SIDE * SIDE
SEQ = PADDED // 2
SCALE = SEQ**-0.5
ORDER = (4, 3, 5, 2, 6, 1, 7)


def split(table):
    high = table.astype(ml_dtypes.bfloat16)
    low = (table - high.astype(np.float64)).astype(ml_dtypes.bfloat16)
    return high, low


def tables():
    half = np.arange(64) + 0.5
    block = 2 * math.pi * np.outer(half, np.arange(64)) / SIDE
    first = np.concatenate([np.cos(block), -np.sin(block)], axis=0)
    first = np.concatenate(split(first), axis=1)
    twist = 2 * math.pi * np.outer(half, np.arange(SIDE)) / PADDED
    twist = np.concatenate([np.cos(twist), np.sin(twist)], axis=0).astype(np.float32)
    inner = 2 * math.pi * np.outer(np.arange(SIDE), np.arange(SIDE)) / SIDE
    c, s = np.cos(inner), np.sin(inner)
    forward = np.block([[c, -s], [s, c]])
    inverse = np.block([[c, s], [-s, c]])
    second = np.concatenate(split(forward) + split(inverse), axis=0)
    last = np.concatenate([np.cos(block.T), -np.sin(block.T)], axis=1) * (2.0 / PADDED)
    high, low = split(last)
    last = np.concatenate([high, high, low], axis=1)
    return first, twist, second, last


def dot(a, b):
    return jnp.dot(a, b, preferred_element_type=F32)


def halves(x):
    high = x.astype(BF16)
    return high, (x - high.astype(F32)).astype(BF16)


def kernel(
    tok, vw, gw, fil, cot, t_first, t_twist, t_second, t_last,
    input_grad, filter_grad, vw_grad, gw_grad,
    s_e, s_l, r1_e, r1_l, r2_e, r2_l, u_e, u_l, w_vg, w_f,
    spec, lhs, mid, s3, r3, r3s, r4, s3f, r3f, s4f, r4f,
    tk, g_all, part, r5, s6, r6, vt, gt, s7, r7, s8, r8,
    sem_qe, sem_ql, sem_ze, sem_zl, sem_zv, sem_zf, sem_qv, sem_qf, sem_q6,
    sem_tk, sem_sib, sem_rs, sem_c7, sem_x8, sem_own,
):
    i = lax.axis_index("seq")
    c = lax.axis_index("ch")
    z, q = i // 8, i % 8
    core, xh = c % 2, c // 2
    sib = c + 1 - 2 * core
    opp = (c + 2) % 4

    def along_z(zz):
        return (zz * 8 + q, c)

    def along_q(qq):
        return (z * 8 + qq, c)

    barrier = pltpu.get_barrier_semaphore()
    peers = 0
    for d in range(1, 8):
        for who in (along_z((z + d) % 8), along_q((q + d) % 8), (((z + d) % 8) * 8 + q, sib)):
            pl.semaphore_signal(barrier, inc=1, device_id=who, device_id_type=MESH)
            peers += 1
    for who in ((i, sib), (i, opp)):
        pl.semaphore_signal(barrier, inc=1, device_id=who, device_id_type=MESH)
        peers += 1

    def pair(a, b):
        a = a.T.reshape(16, 8, SIDE)
        b = b.T.reshape(16, 8, SIDE)
        return jnp.concatenate([a, b], axis=1).astype(BF16).reshape(2, SIDE, SIDE)

    pending = []

    def send(src, dst, ssem, rsem, who):
        copy = pltpu.make_async_remote_copy(
            src_ref=src, dst_ref=dst, send_sem=ssem, recv_sem=rsem, device_id=who, device_id_type=MESH
        )
        copy.start()
        pending.append(copy)

    def arrived(dst, sem, who):
        pltpu.make_async_remote_copy(
            src_ref=dst, dst_ref=dst, send_sem=sem.at[0, 0], recv_sem=sem.at[1, who],
            device_id=(i, sib), device_id_type=MESH,
        ).wait_recv()

    def exchange(me, reach, source, landing, sem):
        for d in ORDER:
            peer = (me + d) % 8
            send(source(peer), landing(me), sem.at[0, d], sem.at[1, me], reach(peer))

    def collect(me, landing, sem):
        for d in ORDER:
            peer = (me + d) % 8
            arrived(landing(peer), sem, peer)

    def rows16(ref, at):
        return ref.at[:, pl.ds(pl.multiple_of(at * 16, 16), 16), :]

    for b in range(4):
        lanes = slice(b * SIDE, (b + 1) * SIDE)
        s_e[2 * b : 2 * b + 2] = pair(fil[:, lanes], cot[:, lanes].astype(F32))
    own_cols = pl.ds(pl.multiple_of(core * 1024, 1024), 1024)
    own = pltpu.make_async_copy(tok.at[:, own_cols], tk.at[q], sem_own)
    own.start()

    pl.semaphore_wait(barrier, peers)
    exchange(q, along_q, lambda p: s_e.at[p], lambda p: r1_e.at[p], sem_qe)
    r1_e[pl.ds(q, 1)] = s_e[pl.ds(q, 1)]

    for b in range(2):
        lanes = slice(b * 256, (b + 1) * 256)
        val = dot(tok[...], vw[:, lanes])
        up = dot(tok[...], gw[:, lanes]) * cot[:, lanes].astype(F32)
        for e in range(2):
            part_lanes = slice(e * SIDE, (e + 1) * SIDE)
            at = 4 * b + 2 * e
            s_l[at : at + 2] = pair(val[:, part_lanes], up[:, part_lanes])
    exchange(q, along_q, lambda p: s_l.at[p], lambda p: r1_l.at[p], sem_ql)
    r1_l[pl.ds(q, 1)] = s_l[pl.ds(q, 1)]

    def second_phase(r1, r2, sem_q, sem_z):
        collect(q, lambda p: r1.at[p], sem_q)
        exchange(z, along_z, lambda p: rows16(r1, p), lambda p: r2.at[p], sem_z)
        mine = r1[:, pl.ds(pl.multiple_of(z * 16, 16), 16), :]
        r2[pl.ds(z, 1)] = mine.reshape(1, 8, 16, SIDE)

    second_phase(r1_e, r2_e, sem_qe, sem_ze)
    for d in ORDER:
        peer = (q + d) % 8
        send(tok.at[:, own_cols], tk.at[q], sem_tk.at[0, d], sem_tk.at[1, q], along_q(peer))
    second_phase(r1_l, r2_l, sem_ql, sem_zl)

    cw = t_twist[0:64]
    sw = t_twist[64:128]
    g_high, g_low, i_high, i_low = (t_second[256 * t : 256 * (t + 1)] for t in range(4))

    def put(at, x):
        high, low = halves(x)
        lhs[0, at * 64 : (at + 1) * 64] = high
        lhs[1, at * 64 : (at + 1) * 64] = low

    def widen(r2, u):
        for zz in range(8):
            u[zz * SIDE : (zz + 1) * SIDE] = r2[zz].reshape(SIDE, SIDE).astype(F32)

    def forward(u, base, out):
        for r in range(0, 8, 2):
            x = [u[pl.ds(base + r + e, 64, stride=16), :] for e in range(2)]
            x = jnp.concatenate(x, axis=1).astype(BF16)
            a = dot(t_first[...], jnp.concatenate([x, x], axis=0))
            for e in range(2):
                re = a[:64, e * SIDE : (e + 1) * SIDE]
                im = a[64:, e * SIDE : (e + 1) * SIDE]
                put(r + e, jnp.concatenate([re * cw + im * sw, im * cw - re * sw], axis=1))
        spec[out] = dot(lhs[0], g_high) + (dot(lhs[1], g_high) + dot(lhs[0], g_low))

    def inverse(left, right, conjugate, store):
        for r in range(8):
            rows = slice(r * 64, (r + 1) * 64)
            ar, ai = spec[left, rows, :SIDE], spec[left, rows, SIDE:]
            br, bi = spec[right, rows, :SIDE], spec[right, rows, SIDE:]
            if conjugate:
                p = [ar * br + ai * bi, ar * bi - ai * br]
            else:
                p = [ar * br - ai * bi, ar * bi + ai * br]
            put(r, jnp.concatenate(p, axis=1))
        mid[...] = dot(lhs[0], i_high) + (dot(lhs[1], i_high) + dot(lhs[0], i_low))
        for r in range(0, 8, 2):
            cols = []
            for e in range(2):
                rows = slice((r + e) * 64, (r + e + 1) * 64)
                re, im = mid[rows, :SIDE], mid[rows, SIDE:]
                cols.append(jnp.concatenate([re * cw - im * sw, im * cw + re * sw], axis=0))
            high, low = halves(jnp.concatenate(cols, axis=1))
            y = dot(t_last[...], jnp.concatenate([high, low, high], axis=0))
            for e in range(2):
                store(r + e, y[:, e * SIDE : (e + 1) * SIDE])

    collect(z, lambda p: r2_e.at[p], sem_ze)
    widen(r2_e, u_e)
    forward(u_e, 0, 0)
    collect(z, lambda p: r2_l.at[p], sem_zl)
    widen(r2_l, u_l)
    forward(u_l, 8, 2)
    forward(u_l, 0, 1)

    def store_v(r, y):
        w_vg[pl.ds(r, 64, stride=16), :] = y

    def store_g(r, y):
        w_vg[pl.ds(8 + r, 64, stride=16), :] = y * u_e[pl.ds(8 + r, 64, stride=16), :]

    def store_f(r, y):
        w_f[pl.ds(r, 64, stride=8), :] = y

    inverse(0, 2, True, store_v)
    inverse(0, 1, False, store_g)
    for zz in range(8):
        s3[zz] = w_vg[zz * SIDE : (zz + 1) * SIDE].astype(BF16)
    exchange(z, along_z, lambda p: s3.at[p], lambda p: r3.at[p], sem_zv)
    r3[pl.ds(z, 1)] = s3[pl.ds(z, 1)]
    inverse(1, 2, True, store_f)
    for zz in range(8):
        s3f[zz] = w_f[zz * 64 : (zz + 1) * 64].astype(BF16)
    exchange(z, along_z, lambda p: s3f.at[p], lambda p: r3f.at[p], sem_zf)
    r3f[pl.ds(z, 1)] = s3f[pl.ds(z, 1)]

    send(r3.at[z], r3s.at[z], sem_sib.at[0, 0], sem_sib.at[1, z], (i, sib))
    for d in ORDER:
        peer = (z + d) % 8
        arrived(r3.at[peer], sem_zv, peer)
        send(r3.at[peer], r3s.at[peer], sem_sib.at[0, d], sem_sib.at[1, peer], (i, sib))
    exchange(q, along_q, lambda p: rows16(r3, p), lambda p: r4.at[p], sem_qv)
    r4[pl.ds(q, 1)] = r3[:, pl.ds(pl.multiple_of(q * 16, 16), 16), :].reshape(1, 8, 16, SIDE)

    collect(q, lambda p: tk.at[p], sem_tk)
    own.wait()
    for qq in range(8):
        g_all[0:SIDE, qq * SIDE : (qq + 1) * SIDE] = r3[:, qq * 16 : (qq + 1) * 16, :].reshape(SIDE, SIDE)
    for d in ORDER + (0,):
        arrived(r3s.at[(z + d) % 8], sem_sib, (z + d) % 8)
    for qq in range(8):
        g_all[SIDE:, qq * SIDE : (qq + 1) * SIDE] = r3s[:, qq * 16 : (qq + 1) * 16, :].reshape(SIDE, SIDE)
    for t in range(4):
        block = tk[:, :, t * 256 : (t + 1) * 256].reshape(1024, 256)
        sums = dot(g_all[...], block).astype(BF16)
        part[t, 0] = sums[:SIDE]
        part[t, 1] = sums[SIDE:]
        to = core * 4 + t

        def share(s, who, t=t, to=to):
            return pltpu.make_async_remote_copy(
                src_ref=part.at[t, s], dst_ref=r5.at[z], send_sem=sem_rs.at[0, 2 * t + s],
                recv_sem=sem_rs.at[1, z], device_id=(to * 8 + q, who), device_id_type=MESH,
            )

        share(1, sib).start()

        @pl.when(to != z)
        def _():
            share(0, c).start()

        @pl.when(to == z)
        def _():
            r5[pl.ds(z, 1)] = part[t, 0].reshape(1, SIDE, 256)

    collect(q, lambda p: r4.at[p], sem_qv)
    for qq in range(8):
        x = r4[qq].astype(F32)
        vt[:, qq * 64 : (qq + 1) * 64] = x[:, :8].reshape(64, SIDE).T.astype(BF16)
        gt[:, qq * 64 : (qq + 1) * 64] = x[:, 8:].reshape(64, SIDE).T.astype(BF16)

    def columns(k):
        rows = pl.ds(pl.multiple_of(k * 512, 512), 512)
        over = (((1,), (1,)), ((), ()))
        a = lax.dot_general(vt[...], vw[rows, :], over, preferred_element_type=F32)
        return a + lax.dot_general(gt[...], gw[rows, :], over, preferred_element_type=F32)

    s7[0] = columns(2 * (1 - xh) + 1 - core)
    s7[1] = columns(2 * xh + 1 - core)
    send(s7, r7, sem_c7.at[0, 0], sem_c7.at[1, 0], (i, sib))
    far = columns(2 * (1 - xh) + core)
    near = columns(2 * xh + core)
    arrived(r7, sem_c7, 0)
    s8[...] = (far + r7[0]).astype(BF16)
    send(s8, r8, sem_x8.at[0, 0], sem_x8.at[1, 0], (i, opp))
    near = near + r7[1]

    collect(z, lambda p: r3f.at[p], sem_zf)
    x = r3f[...].astype(F32).reshape(8, 8, 8, SIDE)
    for qq in range(8):
        s4f[qq] = x[:, qq].reshape(64, SIDE).astype(BF16)
    exchange(q, along_q, lambda p: s4f.at[p], lambda p: r4f.at[p], sem_qf)
    r4f[pl.ds(q, 1)] = s4f[pl.ds(q, 1)]

    for d in ORDER:
        peer = (z + d) % 8
        arrived(r5.at[peer], sem_rs, peer)

    @pl.when(core != z // 4)
    def _():
        arrived(r5.at[z], sem_rs, z)

    total = r5[0].astype(F32)
    for zz in range(1, 8):
        total = total + r5[zz].astype(F32)
    total = total.reshape(8, 2, 8, 256)
    total = jnp.concatenate([total[:, 0].reshape(64, 256), total[:, 1].reshape(64, 256)], axis=0)
    s6[...] = (total.T * SCALE).reshape(8, 32, SIDE)
    exchange(q, along_q, lambda p: s6.at[p], lambda p: r6.at[p], sem_q6)
    r6[pl.ds(q, 1)] = s6[pl.ds(q, 1)]

    arrived(r8, sem_x8, 0)
    input_grad[...] = (near + r8[...].astype(F32)).astype(BF16)

    collect(q, lambda p: r4f.at[p], sem_qf)
    for b in range(4):
        x = r4f[2 * b : 2 * b + 2].astype(F32).reshape(SIDE, SIDE)
        filter_grad[:, b * SIDE : (b + 1) * SIDE] = x.T * SCALE

    collect(q, lambda p: r6.at[p], sem_q6)
    for qq in range(8):
        vw_grad[:, qq * 64 : (qq + 1) * 64] = r6[qq, :, :64]
        gw_grad[:, qq * 64 : (qq + 1) * 64] = r6[qq, :, 64:]

    for copy in pending:
        copy.wait_send()
    for t in range(4):
        for s in range(2):
            copy = pltpu.make_async_remote_copy(
                src_ref=part.at[t, s], dst_ref=r5.at[z], send_sem=sem_rs.at[0, 2 * t + s],
                recv_sem=sem_rs.at[1, z], device_id=(i, sib), device_id_type=MESH,
            )
            if s == 1:
                copy.wait_send()
            else:

                @pl.when(core * 4 + t != z)
                def _(copy=copy):
                    copy.wait_send()


def local(tokens, value_weight, gate_weight, filters, cotangent):
    def v(*shape, dtype=BF16):
        return pltpu.VMEM(shape, dtype)

    sem = pltpu.SemaphoreType.DMA((2, 8))
    vmem = pl.BlockSpec(memory_space=pltpu.VMEM)
    shape = jax.ShapeDtypeStruct
    return pl.pallas_call(
        kernel,
        out_shape=(
            shape((128, 512), BF16),
            shape((128, 512), F32),
            shape((32, 512), F32),
            shape((32, 512), F32),
        ),
        in_specs=[vmem] * 9,
        out_specs=(vmem,) * 4,
        scratch_shapes=[
            v(8, 128, 128), v(8, 128, 128), v(8, 128, 128), v(8, 128, 128),
            v(8, 8, 16, 128), v(8, 8, 16, 128),
            v(1024, 128, dtype=F32), v(1024, 128, dtype=F32), v(1024, 128, dtype=F32), v(512, 128, dtype=F32),
            v(3, 512, 256, dtype=F32), v(2, 512, 256), v(512, 256, dtype=F32),
            v(8, 128, 128), v(8, 128, 128), v(8, 128, 128), v(8, 8, 16, 128),
            v(8, 64, 128), v(8, 64, 128), v(8, 64, 128), v(8, 64, 128),
            v(8, 128, 1024), v(256, 1024), v(4, 2, 128, 256), v(8, 128, 256),
            v(8, 32, 128, dtype=F32), v(8, 32, 128, dtype=F32),
            v(128, 512), v(128, 512),
            v(2, 128, 512, dtype=F32), v(2, 128, 512, dtype=F32), v(128, 512), v(128, 512),
        ] + [sem] * 14 + [pltpu.SemaphoreType.DMA],
        compiler_params=pltpu.CompilerParams(
            collective_id=0, has_side_effects=True, vmem_limit_bytes=48 * 1024 * 1024
        ),
        cost_estimate=pl.CostEstimate(flops=3_000_000_000, bytes_accessed=8_000_000, transcendentals=0),
    )(tokens, value_weight, gate_weight, filters, cotangent, *(jnp.asarray(t) for t in tables()))


def solution(mesh):
    placed = (P("seq", None), P(None, "ch"), P(None, "ch"), P("seq", "ch"), P("seq", "ch"))
    return jax.shard_map(
        local,
        mesh=mesh,
        in_specs=placed,
        out_specs=(P("seq", "ch"),) * 4,
        check_vma=False,
    )
```

time: 705 us -> 78.8 us (0.11)
  the two profiles are of different devices: /device:TPU:4 before, /device:TPU:68 now
where the time goes in v1:
time: 78.8 us; the launch traced here: 78.4 us
  Pallas kernels  67.2 us (85%)
  local copies, waits for them, and re-layouts  10.5 us (13%)
    pallas_call x1, Pallas kernels, local(): pl.pallas_call(kernel, out_shape=(shape((128, 512), BF16), shape((128, 51...  67.2 us
    unnamed x20, local copies, waits for them, and re-layouts  10.5 us

profile of v1, /device:TPU:68, one launch (start us, length us, event | category | flops | bytes accessed | tf_op | source)
XLA Modules:
  0.0 78.4 jit_solution(5016327013646890195)
XLA Ops:
  0.6 0.0 copy-start
  0.6 1.6 %copy-done = bf16[2048,512]{1,0:T(8,128)(2,1)S(1)} copy-done((bf16[2048,512]{1,0:T(8,128)(2,1)S(1)}, bf16[2048,512]{1,0:T(8,128)(2,1)}, u32[]{:S(2)}) %copy-start) | copy-done | bytes 2097176
  2.2 0.0 copy-start.1
  2.2 1.0 %copy-done.1 = bf16[128,2048]{1,0:T(8,128)(2,1)S(1)} copy-done((bf16[128,2048]{1,0:T(8,128)(2,1)S(1)}, bf16[128,2048]{1,0:T(8,128)(2,1)}, u32[]{:S(2)}) %copy-start.1) | copy-done | bytes 524312
  3.3 0.0 copy-start.2
  3.3 0.9 %copy-done.2 = f32[128,512]{1,0:T(8,128)S(1)} copy-done((f32[128,512]{1,0:T(8,128)S(1)}, f32[128,512]{1,0:T(8,128)}, u32[]{:S(2)}) %copy-start.2) | copy-done | bytes 262168
  4.2 0.0 copy-start.3
  4.2 0.9 %copy-done.3 = bf16[128,512]{1,0:T(8,128)(2,1)S(1)} copy-done((bf16[128,512]{1,0:T(8,128)(2,1)S(1)}, bf16[128,512]{1,0:T(8,128)(2,1)}, u32[]{:S(2)}) %copy-start.3) | copy-done | bytes 131096
  5.1 0.0 copy-start.4
  5.1 1.0 %copy-done.4 = bf16[1024,256]{1,0:T(8,128)(2,1)S(1)} copy-done((bf16[1024,256]{1,0:T(8,128)(2,1)S(1)}, bf16[1024,256]{1,0:T(8,128)(2,1)}, u32[]{:S(2)}) %copy-start.4) | copy-done | bytes 524312
  6.2 0.0 copy-start.5
  6.2 0.8 %copy-done.5 = f32[128,128]{1,0:T(8,128)S(1)} copy-done((f32[128,128]{1,0:T(8,128)S(1)}, f32[128,128]{1,0:T(8,128)}, u32[]{:S(2)}) %copy-start.5) | copy-done | bytes 65560
  7.0 0.0 copy-start.6
  7.0 0.8 %copy-done.6 = bf16[64,384]{1,0:T(8,128)(2,1)S(1)} copy-done((bf16[64,384]{1,0:T(8,128)(2,1)S(1)}, bf16[64,384]{1,0:T(8,128)(2,1)}, u32[]{:S(2)}) %copy-start.6) | copy-done | bytes 49176
  7.8 0.0 copy-start.7
  7.8 0.8 copy-done.7
  8.6 67.2 %shard_map.120 = (bf16[128,512]{1,0:T(8,128)(2,1)S(1)}, f32[128,512]{1,0:T(8,128)S(1)}, f32[32,512]{1,0:T(8,128)S(1)}, f32[32,512]{1,0:T(8,128)S(1)}) custom-call(bf16[128,2048]{1,0:T(8,128)(2,1)S(1)} %copy-done.1, bf16[2048,512]{1,0:T(8,128)(2,1)S(1)} %copy-done, bf16[2048,512]{1,0:T(8,128)(2,1)} %gw.1, f32[128,512]{1,0:T(8,128)S(1)} %copy-done.2, ...), custom_call_target="tpu_custom_call" | custom-call | flops 3000000000 | bytes 8000000 | tf_op jit(solution)/shard_map/pallas_call | solution.py:352
  75.8 0.7 copy.17
  76.4 0.7 copy.18
  77.1 0.6 copy.19
  77.7 0.6 copy.20
Async XLA Ops:
  0.6 1.6 %copy-start = (bf16[2048,512]{1,0:T(8,128)(2,1)S(1)}, bf16[2048,512]{1,0:T(8,128)(2,1)}, u32[]{:S(2)}) copy-start(bf16[2048,512]{1,0:T(8,128)(2,1)} %vw.1) | copy-start | bytes 6291460
  2.2 1.0 %copy-start.1 = (bf16[128,2048]{1,0:T(8,128)(2,1)S(1)}, bf16[128,2048]{1,0:T(8,128)(2,1)}, u32[]{:S(2)}) copy-start(bf16[128,2048]{1,0:T(8,128)(2,1)} %tok.1) | copy-start | bytes 1572868
  3.3 0.9 %copy-start.2 = (f32[128,512]{1,0:T(8,128)S(1)}, f32[128,512]{1,0:T(8,128)}, u32[]{:S(2)}) copy-start(f32[128,512]{1,0:T(8,128)} %fil.1) | copy-start | bytes 786436
  4.2 0.9 %copy-start.3 = (bf16[128,512]{1,0:T(8,128)(2,1)S(1)}, bf16[128,512]{1,0:T(8,128)(2,1)}, u32[]{:S(2)}) copy-start(bf16[128,512]{1,0:T(8,128)(2,1)} %cot.1) | copy-start | bytes 393220
  5.1 1.0 %copy-start.4 = (bf16[1024,256]{1,0:T(8,128)(2,1)S(1)}, bf16[1024,256]{1,0:T(8,128)(2,1)}, u32[]{:S(2)}) copy-start(bf16[1024,256]{1,0:T(8,128)(2,1)} %constant.10.clone.t_second) | copy-start | bytes 1572868
  6.2 0.8 %copy-start.5 = (f32[128,128]{1,0:T(8,128)S(1)}, f32[128,128]{1,0:T(8,128)}, u32[]{:S(2)}) copy-start(f32[128,128]{1,0:T(8,128)} %constant.9.clone.t_twist) | copy-start | bytes 196612
  7.0 0.8 %copy-start.6 = (bf16[64,384]{1,0:T(8,128)(2,1)S(1)}, bf16[64,384]{1,0:T(8,128)(2,1)}, u32[]{:S(2)}) copy-start(bf16[64,384]{1,0:T(8,128)(2,1)} %constant.11.clone.t_last) | copy-start | bytes 147460
  7.8 0.8 copy-start.7

commit v2 on v1

--- a/solution.py
+++ b/solution.py
@@ -41,7 +41,7 @@
     last = np.concatenate([np.cos(block.T), -np.sin(block.T)], axis=1) * (2.0 / PADDED)
     high, low = split(last)
     last = np.concatenate([high, high, low], axis=1)
-    return first, twist, second, last
+    return tuple(t.astype(np.float32) for t in (first, twist, second, last))
 
 
 def dot(a, b):
@@ -54,13 +54,14 @@
 
 
 def kernel(
+    tok_in, vw_in, gw_in, fil_in, cot_in, t_first_in, t_twist_in, t_second_in, t_last_in,
+    input_grad, filter_grad, vw_grad, gw_grad,
     tok, vw, gw, fil, cot, t_first, t_twist, t_second, t_last,
-    input_grad, filter_grad, vw_grad, gw_grad,
-    s_e, s_l, r1_e, r1_l, r2_e, r2_l, u_e, u_l, w_vg, w_f,
+    t_first16, t_second16, t_last16, s_e, s_l, r1_e, r1_l, r2_e, r2_l, u_e, u_l, w_vg, w_f,
     spec, lhs, mid, s3, r3, r3s, r4, s3f, r3f, s4f, r4f,
     tk, g_all, part, r5, s6, r6, vt, gt, s7, r7, s8, r8,
     sem_qe, sem_ql, sem_ze, sem_zl, sem_zv, sem_zf, sem_qv, sem_qf, sem_q6,
-    sem_tk, sem_sib, sem_rs, sem_c7, sem_x8, sem_own,
+    sem_tk, sem_sib, sem_rs, sem_c7, sem_x8, sem_own, sem_in,
 ):
     i = lax.axis_index("seq")
     c = lax.axis_index("ch")
@@ -74,6 +75,23 @@
 
     def along_q(qq):
         return (z * 8 + qq, c)
+
+    loads = {}
+    for at, (name, src, dst) in enumerate(
+        (
+            ("fil", fil_in, fil),
+            ("cot", cot_in, cot),
+            ("tok", tok_in, tok),
+            ("vw", vw_in, vw),
+            ("gw", gw_in, gw),
+            ("first", t_first_in, t_first),
+            ("twist", t_twist_in, t_twist),
+            ("second", t_second_in, t_second),
+            ("last", t_last_in, t_last),
+        )
+    ):
+        loads[name] = pltpu.make_async_copy(src, dst, sem_in.at[at])
+        loads[name].start()
 
     barrier = pltpu.get_barrier_semaphore()
     peers = 0
@@ -118,9 +136,12 @@
     def rows16(ref, at):
         return ref.at[:, pl.ds(pl.multiple_of(at * 16, 16), 16), :]
 
+    loads["fil"].wait()
+    loads["cot"].wait()
     for b in range(4):
         lanes = slice(b * SIDE, (b + 1) * SIDE)
         s_e[2 * b : 2 * b + 2] = pair(fil[:, lanes], cot[:, lanes].astype(F32))
+    loads["tok"].wait()
     own_cols = pl.ds(pl.multiple_of(core * 1024, 1024), 1024)
     own = pltpu.make_async_copy(tok.at[:, own_cols], tk.at[q], sem_own)
     own.start()
@@ -129,6 +150,8 @@
     exchange(q, along_q, lambda p: s_e.at[p], lambda p: r1_e.at[p], sem_qe)
     r1_e[pl.ds(q, 1)] = s_e[pl.ds(q, 1)]
 
+    loads["vw"].wait()
+    loads["gw"].wait()
     for b in range(2):
         lanes = slice(b * 256, (b + 1) * 256)
         val = dot(tok[...], vw[:, lanes])
@@ -146,16 +169,22 @@
         mine = r1[:, pl.ds(pl.multiple_of(z * 16, 16), 16), :]
         r2[pl.ds(z, 1)] = mine.reshape(1, 8, 16, SIDE)
 
+    for name in ("first", "twist", "second", "last"):
+        loads[name].wait()
+    cw = t_twist[0:64]
+    sw = t_twist[64:128]
+    for t in range(4):
+        t_second16[t] = t_second[256 * t : 256 * (t + 1)].astype(BF16)
+    t_first16[...] = t_first[...].astype(BF16)
+    t_last16[...] = t_last[...].astype(BF16)
+    g_high, g_low, i_high, i_low = (t_second16[t] for t in range(4))
+
     second_phase(r1_e, r2_e, sem_qe, sem_ze)
     for d in ORDER:
         peer = (q + d) % 8
         send(tok.at[:, own_cols], tk.at[q], sem_tk.at[0, d], sem_tk.at[1, q], along_q(peer))
     second_phase(r1_l, r2_l, sem_ql, sem_zl)
 
-    cw = t_twist[0:64]
-    sw = t_twist[64:128]
-    g_high, g_low, i_high, i_low = (t_second[256 * t : 256 * (t + 1)] for t in range(4))
-
     def put(at, x):
         high, low = halves(x)
         lhs[0, at * 64 : (at + 1) * 64] = high
@@ -169,7 +198,7 @@
         for r in range(0, 8, 2):
             x = [u[pl.ds(base + r + e, 64, stride=16), :] for e in range(2)]
             x = jnp.concatenate(x, axis=1).astype(BF16)
-            a = dot(t_first[...], jnp.concatenate([x, x], axis=0))
+            a = dot(t_first16[...], jnp.concatenate([x, x], axis=0))
             for e in range(2):
                 re = a[:64, e * SIDE : (e + 1) * SIDE]
                 im = a[64:, e * SIDE : (e + 1) * SIDE]
@@ -194,7 +223,7 @@
                 re, im = mid[rows, :SIDE], mid[rows, SIDE:]
                 cols.append(jnp.concatenate([re * cw - im * sw, im * cw + re * sw], axis=0))
             high, low = halves(jnp.concatenate(cols, axis=1))
-            y = dot(t_last[...], jnp.concatenate([high, low, high], axis=0))
+            y = dot(t_last16[...], jnp.concatenate([high, low, high], axis=0))
             for e in range(2):
                 store(r + e, y[:, e * SIDE : (e + 1) * SIDE])
 
@@ -348,8 +377,11 @@
 
     sem = pltpu.SemaphoreType.DMA((2, 8))
     vmem = pl.BlockSpec(memory_space=pltpu.VMEM)
+    whole = pl.BlockSpec(memory_space=pl.ANY)
+    operands = [tokens, value_weight, gate_weight, filters, cotangent]
+    operands += [jnp.asarray(t) for t in tables()]
     shape = jax.ShapeDtypeStruct
-    return pl.pallas_call(
+    results = pl.pallas_call(
         kernel,
         out_shape=(
             shape((128, 512), BF16),
@@ -357,9 +389,10 @@
             shape((32, 512), F32),
             shape((32, 512), F32),
         ),
-        in_specs=[vmem] * 9,
+        in_specs=[whole] * 9,
         out_specs=(vmem,) * 4,
-        scratch_shapes=[
+        scratch_shapes=[pltpu.VMEM(t.shape, t.dtype) for t in operands] + [
+            v(128, 128), v(4, 256, 256), v(64, 384),
             v(8, 128, 128), v(8, 128, 128), v(8, 128, 128), v(8, 128, 128),
             v(8, 8, 16, 128), v(8, 8, 16, 128),
             v(1024, 128, dtype=F32), v(1024, 128, dtype=F32), v(1024, 128, dtype=F32), v(512, 128, dtype=F32),
@@ -370,12 +403,28 @@
             v(8, 32, 128, dtype=F32), v(8, 32, 128, dtype=F32),
             v(128, 512), v(128, 512),
             v(2, 128, 512, dtype=F32), v(2, 128, 512, dtype=F32), v(128, 512), v(128, 512),
-        ] + [sem] * 14 + [pltpu.SemaphoreType.DMA],
+        ] + [sem] * 14 + [pltpu.SemaphoreType.DMA, pltpu.SemaphoreType.DMA((9,))],
         compiler_params=pltpu.CompilerParams(
-            collective_id=0, has_side_effects=True, vmem_limit_bytes=48 * 1024 * 1024
+            collective_id=0, has_side_effects=True, vmem_limit_bytes=60 * 1024 * 1024
         ),
         cost_estimate=pl.CostEstimate(flops=3_000_000_000, bytes_accessed=8_000_000, transcendentals=0),
-    )(tokens, value_weight, gate_weight, filters, cotangent, *(jnp.asarray(t) for t in tables()))
+    )(*operands)
+    return pl.pallas_call(
+        hand_over,
+        out_shape=tuple(shape(r.shape, r.dtype) for r in results),
+        in_specs=[whole] * 4,
+        out_specs=(whole,) * 4,
+        scratch_shapes=[pltpu.SemaphoreType.DMA((4,))],
+        compiler_params=pltpu.CompilerParams(vmem_limit_bytes=60 * 1024 * 1024),
+    )(*results)
+
+
+def hand_over(*refs):
+    copies = [pltpu.make_async_copy(refs[t], refs[4 + t], refs[8].at[t]) for t in range(4)]
+    for copy in copies:
+        copy.start()
+    for copy in copies:
+        copy.wait()
 
 
 def solution(mesh):

time: 78.8 us -> 84.3 us (1.070)
  Pallas kernels: 67.2 us -> 83.6 us
  local copies, waits for them, and re-layouts: 10.5 us -> 0 us
    pallas_call x0 -> x1, Pallas kernels: none -> 17 us  [local(): pl.pallas_call(hand_over, out_shape=tuple((shape(r.shape, r.dtype) for r...]
    unnamed x20 -> x0, local copies, waits for them, and re-layouts: 10.5 us -> none
where the time goes in v2:
time: 84.3 us; the launch traced here: 84.2 us
  Pallas kernels  83.6 us (99%)
    pallas_call x1, Pallas kernels, local(): pl.pallas_call(kernel, out_shape=(shape((128, 512), BF16), shape((128, 51...  66.6 us
    pallas_call x1, Pallas kernels, local(): pl.pallas_call(hand_over, out_shape=tuple((shape(r.shape, r.dtype) for r...  17 us

profile of v2, /device:TPU:68, one launch (start us, length us, event | category | flops | bytes accessed | tf_op | source)
XLA Modules:
  0.0 84.2 jit_solution(17097028010654933562)
XLA Ops:
  0.6 66.6 %shard_map.120 = (bf16[128,512]{1,0:T(8,128)(2,1)}, f32[128,512]{1,0:T(8,128)}, f32[32,512]{1,0:T(8,128)}, f32[32,512]{1,0:T(8,128)}) custom-call(bf16[128,2048]{1,0:T(8,128)(2,1)} %tok_in.1, bf16[2048,512]{1,0:T(8,128)(2,1)} %vw_in.1, bf16[2048,512]{1,0:T(8,128)(2,1)} %gw_in.1, f32[128,512]{1,0:T(8,128)} %fil_in.1, bf16[128,512]{1,0:T(8,128)(2,1)} %cot_in.1, ...), custom_call_target="tpu_custom_call" | custom-call | flops 3000000000 | bytes 8000000 | tf_op jit(solution)/shard_map/pallas_call | solution.py:384
  67.2 17.0 %shard_map.121 = (bf16[128,512]{1,0:T(8,128)(2,1)}, f32[128,512]{1,0:T(8,128)}, f32[32,512]{1,0:T(8,128)}, f32[32,512]{1,0:T(8,128)}) custom-call(bf16[128,512]{1,0:T(8,128)(2,1)} %get-tuple-element.8.refs_0_, f32[128,512]{1,0:T(8,128)} %get-tuple-element.9.refs_1_, f32[32,512]{1,0:T(8,128)} %get-tuple-element.10.refs_2_, f32[32,512]{1,0:T(8,128)} %get-tuple-element.11.refs_3_), custom_call_target="tpu_custom_call" | custom-call | tf_op jit(solution)/shard_map/pallas_call | solution.py:412

commit v3 on v2

--- a/solution.py
+++ b/solution.py
@@ -18,6 +18,9 @@
 SEQ = PADDED // 2
 SCALE = SEQ**-0.5
 ORDER = (4, 3, 5, 2, 6, 1, 7)
+NEAR = ((0, 0), (1, 0), (0, 1), (0, 3), (1, 1), (1, 3), (0, 2), (1, 2))
+BACK = (0, 1, 3, 2, 5, 4, 6, 7)
+GROUPS = ((0, 1), (1, 4), (4, 8))
 
 
 def split(table):
@@ -76,6 +79,10 @@
     def along_q(qq):
         return (z * 8 + qq, c)
 
+    def near(slot):
+        dx, dy = NEAR[slot]
+        return (q // 4 + dx) % 2 * 4 + (q + dy) % 4
+
     loads = {}
     for at, (name, src, dst) in enumerate(
         (
@@ -147,8 +154,15 @@
     own.start()
 
     pl.semaphore_wait(barrier, peers)
-    exchange(q, along_q, lambda p: s_e.at[p], lambda p: r1_e.at[p], sem_qe)
-    r1_e[pl.ds(q, 1)] = s_e[pl.ds(q, 1)]
+    exchange(z, along_z, lambda p: rows16(s_e, p), lambda p: r1_e.at[p], sem_ze)
+    r1_e[pl.ds(z, 1)] = s_e[:, pl.ds(pl.multiple_of(z * 16, 16), 16), :].reshape(1, 8, 16, SIDE)
+
+    def give(src, dst, at, slot):
+        send(src, dst, sem_tk.at[0, at], sem_tk.at[1, at], along_q(near(slot)))
+
+    half = tok.at[:, own_cols]
+    for at, slot in ((0, 1), (1, 3), (2, 2)):
+        give(half, tk.at[q], at, slot)
 
     loads["vw"].wait()
     loads["gw"].wait()
@@ -160,15 +174,28 @@
             part_lanes = slice(e * SIDE, (e + 1) * SIDE)
             at = 4 * b + 2 * e
             s_l[at : at + 2] = pair(val[:, part_lanes], up[:, part_lanes])
-    exchange(q, along_q, lambda p: s_l.at[p], lambda p: r1_l.at[p], sem_ql)
-    r1_l[pl.ds(q, 1)] = s_l[pl.ds(q, 1)]
-
-    def second_phase(r1, r2, sem_q, sem_z):
-        collect(q, lambda p: r1.at[p], sem_q)
-        exchange(z, along_z, lambda p: rows16(r1, p), lambda p: r2.at[p], sem_z)
-        mine = r1[:, pl.ds(pl.multiple_of(z * 16, 16), 16), :]
-        r2[pl.ds(z, 1)] = mine.reshape(1, 8, 16, SIDE)
-
+    for slot in range(1, 8):
+        send(
+            s_l.at[near(slot)], r1_l.at[BACK[slot]],
+            sem_ql.at[0, slot], sem_ql.at[1, BACK[slot]], along_q(near(slot)),
+        )
+    r1_l[0] = s_l[pl.ds(q, 1)].reshape(SIDE, SIDE)
+
+    def onward(group):
+        a, b = GROUPS[group]
+        for slot in range(max(a, 1), b):
+            arrived(r1_l.at[slot], sem_ql, slot)
+        for d in ORDER:
+            peer = (z + d) % 8
+            rows = pl.ds(pl.multiple_of(peer * 16, 16), 16)
+            send(
+                r1_l.at[a:b, rows, :], r2_l.at[z, a:b],
+                sem_zl.at[0, 8 * group + d], sem_zl.at[1, 8 * group + z], along_z(peer),
+            )
+        mine = r1_l[a:b, pl.ds(pl.multiple_of(z * 16, 16), 16), :]
+        r2_l[pl.ds(z, 1), a:b] = mine.reshape(1, b - a, 16, SIDE)
+
+    onward(0)
     for name in ("first", "twist", "second", "last"):
         loads[name].wait()
     cw = t_twist[0:64]
@@ -179,20 +206,19 @@
     t_last16[...] = t_last[...].astype(BF16)
     g_high, g_low, i_high, i_low = (t_second16[t] for t in range(4))
 
-    second_phase(r1_e, r2_e, sem_qe, sem_ze)
-    for d in ORDER:
-        peer = (q + d) % 8
-        send(tok.at[:, own_cols], tk.at[q], sem_tk.at[0, d], sem_tk.at[1, q], along_q(peer))
-    second_phase(r1_l, r2_l, sem_ql, sem_zl)
+    collect(z, lambda p: r1_e.at[p], sem_ze)
+    exchange(q, along_q, lambda p: r1_e.at[:, p], lambda p: r2_e.at[:, p], sem_qe)
+    r2_e[:, pl.ds(q, 1)] = r1_e[:, pl.ds(q, 1)]
+    onward(1)
+    onward(2)
+    arrived(tk.at[near(1)], sem_tk, 0)
+    give(tk.at[near(1)], tk.at[near(1)], 3, 3)
+    give(tk.at[near(1)], tk.at[near(1)], 4, 2)
 
     def put(at, x):
         high, low = halves(x)
         lhs[0, at * 64 : (at + 1) * 64] = high
         lhs[1, at * 64 : (at + 1) * 64] = low
-
-    def widen(r2, u):
-        for zz in range(8):
-            u[zz * SIDE : (zz + 1) * SIDE] = r2[zz].reshape(SIDE, SIDE).astype(F32)
 
     def forward(u, base, out):
         for r in range(0, 8, 2):
@@ -227,11 +253,18 @@
             for e in range(2):
                 store(r + e, y[:, e * SIDE : (e + 1) * SIDE])
 
-    collect(z, lambda p: r2_e.at[p], sem_ze)
-    widen(r2_e, u_e)
+    collect(q, lambda p: r2_e.at[:, p], sem_qe)
+    for zz in range(8):
+        u_e[zz * SIDE : (zz + 1) * SIDE] = r2_e[zz].reshape(SIDE, SIDE).astype(F32)
     forward(u_e, 0, 0)
-    collect(z, lambda p: r2_l.at[p], sem_zl)
-    widen(r2_l, u_l)
+    for group, (a, b) in enumerate(GROUPS):
+        for d in ORDER:
+            peer = (z + d) % 8
+            arrived(r2_l.at[peer, a:b], sem_zl, 8 * group + peer)
+        for slot in range(a, b):
+            for zz in range(8):
+                at = pl.multiple_of(zz * SIDE + near(slot) * 16, 16)
+                u_l[pl.ds(at, 16), :] = r2_l[zz, slot].astype(F32)
     forward(u_l, 8, 2)
     forward(u_l, 0, 1)
 
@@ -256,6 +289,13 @@
     exchange(z, along_z, lambda p: s3f.at[p], lambda p: r3f.at[p], sem_zf)
     r3f[pl.ds(z, 1)] = s3f[pl.ds(z, 1)]
 
+    for at, slot in ((1, 2), (2, 3), (3, 4), (4, 5)):
+        arrived(tk.at[near(slot)], sem_tk, at)
+    for at, slot in ((5, 2), (6, 4)):
+        give(tk.at[near(slot), 0:64], tk.at[near(slot), 0:64], at, 3)
+    for at, slot in ((7, 3), (8, 5)):
+        give(tk.at[near(slot), 64:SIDE], tk.at[near(slot), 64:SIDE], at, 2)
+
     send(r3.at[z], r3s.at[z], sem_sib.at[0, 0], sem_sib.at[1, z], (i, sib))
     for d in ORDER:
         peer = (z + d) % 8
@@ -264,7 +304,9 @@
     exchange(q, along_q, lambda p: rows16(r3, p), lambda p: r4.at[p], sem_qv)
     r4[pl.ds(q, 1)] = r3[:, pl.ds(pl.multiple_of(q * 16, 16), 16), :].reshape(1, 8, 16, SIDE)
 
-    collect(q, lambda p: tk.at[p], sem_tk)
+    for at, slot in ((5, 6), (6, 7)):
+        arrived(tk.at[near(slot), 0:64], sem_tk, at)
+        arrived(tk.at[near(slot), 64:SIDE], sem_tk, at + 2)
     own.wait()
     for qq in range(8):
         g_all[0:SIDE, qq * SIDE : (qq + 1) * SIDE] = r3[:, qq * 16 : (qq + 1) * 16, :].reshape(SIDE, SIDE)
@@ -311,11 +353,11 @@
     s7[1] = columns(2 * xh + 1 - core)
     send(s7, r7, sem_c7.at[0, 0], sem_c7.at[1, 0], (i, sib))
     far = columns(2 * (1 - xh) + core)
-    near = columns(2 * xh + core)
+    here = columns(2 * xh + core)
     arrived(r7, sem_c7, 0)
     s8[...] = (far + r7[0]).astype(BF16)
     send(s8, r8, sem_x8.at[0, 0], sem_x8.at[1, 0], (i, opp))
-    near = near + r7[1]
+    here = here + r7[1]
 
     collect(z, lambda p: r3f.at[p], sem_zf)
     x = r3f[...].astype(F32).reshape(8, 8, 8, SIDE)
@@ -342,7 +384,7 @@
     r6[pl.ds(q, 1)] = s6[pl.ds(q, 1)]
 
     arrived(r8, sem_x8, 0)
-    input_grad[...] = (near + r8[...].astype(F32)).astype(BF16)
+    input_grad[...] = (here + r8[...].astype(F32)).astype(BF16)
 
     collect(q, lambda p: r4f.at[p], sem_qf)
     for b in range(4):
@@ -375,7 +417,7 @@
     def v(*shape, dtype=BF16):
         return pltpu.VMEM(shape, dtype)
 
-    sem = pltpu.SemaphoreType.DMA((2, 8))
+    sem = pltpu.SemaphoreType.DMA((2, 24))
     vmem = pl.BlockSpec(memory_space=pltpu.VMEM)
     whole = pl.BlockSpec(memory_space=pl.ANY)
     operands = [tokens, value_weight, gate_weight, filters, cotangent]
@@ -393,7 +435,7 @@
         out_specs=(vmem,) * 4,
         scratch_shapes=[pltpu.VMEM(t.shape, t.dtype) for t in operands] + [
             v(128, 128), v(4, 256, 256), v(64, 384),
-            v(8, 128, 128), v(8, 128, 128), v(8, 128, 128), v(8, 128, 128),
+            v(8, 128, 128), v(8, 128, 128), v(8, 8, 16, 128), v(8, 128, 128),
             v(8, 8, 16, 128), v(8, 8, 16, 128),
             v(1024, 128, dtype=F32), v(1024, 128, dtype=F32), v(1024, 128, dtype=F32), v(512, 128, dtype=F32),
             v(3, 512, 256, dtype=F32), v(2, 512, 256), v(512, 256, dtype=F32),
@@ -414,16 +456,20 @@
         out_shape=tuple(shape(r.shape, r.dtype) for r in results),
         in_specs=[whole] * 4,
         out_specs=(whole,) * 4,
-        scratch_shapes=[pltpu.SemaphoreType.DMA((4,))],
+        scratch_shapes=[pltpu.VMEM(r.shape, r.dtype) for r in results] + [pltpu.SemaphoreType.DMA((8,))],
         compiler_params=pltpu.CompilerParams(vmem_limit_bytes=60 * 1024 * 1024),
     )(*results)
 
 
 def hand_over(*refs):
-    copies = [pltpu.make_async_copy(refs[t], refs[4 + t], refs[8].at[t]) for t in range(4)]
-    for copy in copies:
+    into = [pltpu.make_async_copy(refs[t], refs[8 + t], refs[12].at[t]) for t in range(4)]
+    onto = [pltpu.make_async_copy(refs[8 + t], refs[4 + t], refs[12].at[4 + t]) for t in range(4)]
+    for copy in into:
         copy.start()
-    for copy in copies:
+    for copy, after in zip(into, onto):
+        copy.wait()
+        after.start()
+    for copy in onto:
         copy.wait()
 
 

time: 84.3 us -> 65.8 us (0.78)
  the two profiles are of different devices: /device:TPU:68 before, /device:TPU:64 now
where the time goes in v3:
time: 65.8 us; the launch traced here: 65.7 us
  Pallas kernels  65.1 us (99%)
    pallas_call x1, Pallas kernels, local(): pl.pallas_call(kernel, out_shape=(shape((128, 512), BF16), shape((128, 51...  63.2 us
    pallas_call x1, Pallas kernels, local(): pl.pallas_call(hand_over, out_shape=tuple((shape(r.shape, r.dtype) for r...  1.83 us

profile of v3, /device:TPU:64, one launch (start us, length us, event | category | flops | bytes accessed | tf_op | source)
XLA Modules:
  0.0 65.7 jit_solution(11534458477280431621)
XLA Ops:
  0.6 63.2 %shard_map.120 = (bf16[128,512]{1,0:T(8,128)(2,1)}, f32[128,512]{1,0:T(8,128)}, f32[32,512]{1,0:T(8,128)}, f32[32,512]{1,0:T(8,128)}) custom-call(bf16[128,2048]{1,0:T(8,128)(2,1)} %tok_in.1, bf16[2048,512]{1,0:T(8,128)(2,1)} %vw_in.1, bf16[2048,512]{1,0:T(8,128)(2,1)} %gw_in.1, f32[128,512]{1,0:T(8,128)} %fil_in.1, bf16[128,512]{1,0:T(8,128)(2,1)} %cot_in.1, ...), custom_call_target="tpu_custom_call" | custom-call | flops 3000000000 | bytes 8000000 | tf_op jit(solution)/shard_map/pallas_call | solution.py:426
  63.9 1.8 %shard_map.121 = (bf16[128,512]{1,0:T(8,128)(2,1)}, f32[128,512]{1,0:T(8,128)}, f32[32,512]{1,0:T(8,128)}, f32[32,512]{1,0:T(8,128)}) custom-call(bf16[128,512]{1,0:T(8,128)(2,1)} %get-tuple-element.8.refs_0_, f32[128,512]{1,0:T(8,128)} %get-tuple-element.9.refs_1_, f32[32,512]{1,0:T(8,128)} %get-tuple-element.10.refs_2_, f32[32,512]{1,0:T(8,128)} %get-tuple-element.11.refs_3_), custom_call_target="tpu_custom_call" | custom-call | tf_op jit(solution)/shard_map/pallas_call | solution.py:454

commit v4 on v3

v4 whole, which is shorter than its diff:
```python
import functools
import math

import jax
import jax.numpy as jnp
import ml_dtypes
import numpy as np
from jax import lax
from jax.experimental import pallas as pl
from jax.experimental.pallas import tpu as pltpu
from jax.sharding import PartitionSpec as P

MESH = pl.DeviceIdType.MESH
F32 = jnp.float32
BF16 = jnp.bfloat16
SIDE = 128
PADDED = SIDE * SIDE
SEQ = PADDED // 2
SCALE = SEQ**-0.5
ORDER = (4, 3, 5, 2, 6, 1, 7)
NEAR = ((0, 0), (1, 0), (0, 1), (0, 3), (1, 1), (1, 3), (0, 2), (1, 2))
BACK = (0, 1, 3, 2, 5, 4, 6, 7)
GROUPS = ((0, 1), (1, 4), (4, 8))
CLOSE, FAR = (2, 6, 1, 7), (4, 3, 5)
LOADS = ("fil", "cot", "tok", "vw", "gw", "first", "twist", "second", "last")
OUTGOING = ("ez", "eq", "lq", "lz", "cq", "vz", "sib", "fz", "vq", "fq", "tk", "rs", "core", "far")
INCOMING = (
    "ez", "eq", "lq1", "lq2", "lz0", "lz1", "lz2", "cq", "vzc", "vzf", "sibc", "sibf", "fz", "vq", "fq",
    "tk0", "tk1", "tk2", "rs", "core", "far",
)
SEMAPHORES = (
    tuple(t + ">" for t in OUTGOING)
    + tuple(">" + t for t in INCOMING)
    + ("own", "out0", "out1", "out2", "out3")
    + LOADS
)


def split(table):
    high = table.astype(ml_dtypes.bfloat16)
    low = (table - high.astype(np.float64)).astype(ml_dtypes.bfloat16)
    return high, low


def tables():
    half = np.arange(64) + 0.5
    block = 2 * math.pi * np.outer(half, np.arange(64)) / SIDE
    first = np.concatenate([np.cos(block), -np.sin(block)], axis=0)
    first = np.concatenate(split(first), axis=1)
    twist = 2 * math.pi * np.outer(half, np.arange(SIDE)) / PADDED
    twist = np.concatenate([np.cos(twist), np.sin(twist)], axis=0).astype(np.float32)
    inner = 2 * math.pi * np.outer(np.arange(SIDE), np.arange(SIDE)) / SIDE
    c, s = np.cos(inner), np.sin(inner)
    forward = np.block([[c, -s], [s, c]])
    inverse = np.block([[c, s], [-s, c]])
    second = np.concatenate(split(forward) + split(inverse), axis=0)
    last = np.concatenate([np.cos(block.T), -np.sin(block.T)], axis=1) * (2.0 / PADDED)
    high, low = split(last)
    last = np.concatenate([high, high, low], axis=1)
    return tuple(t.astype(np.float32) for t in (first, twist, second, last))


def dot(a, b):
    return jnp.dot(a, b, preferred_element_type=F32)


def halves(x):
    high = x.astype(BF16)
    return high, (x - high.astype(F32)).astype(BF16)


def kernel(
    tok_in, vw_in, gw_in, fil_in, cot_in, t_first_in, t_twist_in, t_second_in, t_last_in,
    input_grad, filter_grad, vw_grad, gw_grad,
    tok, vw, gw, fil, cot, t_first, t_twist, t_second, t_last,
    t_first16, t_second16, t_last16, s_e, s_l, r1_e, r1_l, s2_e, r2_e, r2_l, u_e, u_l, w_vg, w_f,
    s_c, r_c, wide_c,
    spec, lhs, mid, s3, r3, r3s, r4, s3f, r3f, s4f, r4f,
    tk, g_all, part, r5, vt, gt, s7, r7, s8, r8, o_in, o_fil, o_vw, o_gw, sems,
):
    i = lax.axis_index("seq")
    c = lax.axis_index("ch")
    z, q = i // 8, i % 8
    core, xh = c % 2, c // 2
    sib = c + 1 - 2 * core
    opp = (c + 2) % 4

    def along_z(zz):
        return (zz * 8 + q, c)

    def along_q(qq):
        return (z * 8 + qq, c)

    def near(slot):
        dx, dy = NEAR[slot]
        return (q // 4 + dx) % 2 * 4 + (q + dy) % 4

    def sem(name):
        return sems.at[SEMAPHORES.index(name)]

    loads = {}
    sources = (fil_in, cot_in, tok_in, vw_in, gw_in, t_first_in, t_twist_in, t_second_in, t_last_in)
    places = (fil, cot, tok, vw, gw, t_first, t_twist, t_second, t_last)
    for name, src, dst in zip(LOADS, sources, places):
        loads[name] = pltpu.make_async_copy(src, dst, sem(name))
        loads[name].start()

    barrier = pltpu.get_barrier_semaphore()
    peers = 0
    for d in range(1, 8):
        for who in (along_z((z + d) % 8), along_q((q + d) % 8)):
            pl.semaphore_signal(barrier, inc=1, device_id=who, device_id_type=MESH)
            peers += 1
    for who in ((i, sib), (i, opp), (along_q(near(1))[0], opp)):
        pl.semaphore_signal(barrier, inc=1, device_id=who, device_id_type=MESH)
        peers += 1

    def pair(a, b):
        a = a.T.reshape(16, 8, SIDE)
        b = b.T.reshape(16, 8, SIDE)
        return jnp.concatenate([a, b], axis=1).astype(BF16).reshape(2, SIDE, SIDE)

    def send(src, dst, out, into, who):
        pltpu.make_async_remote_copy(
            src_ref=src, dst_ref=dst, send_sem=sem(out), recv_sem=sem(into), device_id=who, device_id_type=MESH
        ).start()

    def waiter(size, out, into):
        return pltpu.make_async_remote_copy(
            src_ref=size, dst_ref=size, send_sem=sem(out), recv_sem=sem(into),
            device_id=(i, sib), device_id_type=MESH,
        )

    def arrived(size, out, into):
        waiter(size, out, into).wait_recv()

    def rows16(ref, at):
        return ref.at[:, pl.ds(pl.multiple_of(at * 16, 16), 16), :]

    loads["fil"].wait()
    for b in range(4):
        rows = fil[:, b * SIDE : (b + 1) * SIDE].T.reshape(2, 8, 8, SIDE)
        for zz in range(8):
            s_e[zz, b * 16 : (b + 1) * 16] = rows[:, zz].reshape(16, SIDE).astype(BF16)
    loads["tok"].wait()
    own_cols = pl.ds(pl.multiple_of(core * 1024, 1024), 1024)
    half = tok.at[:, own_cols]
    own = pltpu.make_async_copy(half, tk.at[q], sem("own"))
    own.start()

    pl.semaphore_wait(barrier, peers)
    for d in ORDER:
        peer = (z + d) % 8
        send(s_e.at[peer], r1_e.at[z], "ez>", ">ez", along_z(peer))
    r1_e[pl.ds(z, 1)] = s_e[pl.ds(z, 1)]

    loads["cot"].wait()
    loads["vw"].wait()
    loads["gw"].wait()
    for b in range(2):
        lanes = slice(b * 256, (b + 1) * 256)
        val = dot(tok[...], vw[:, lanes])
        up = dot(tok[...], gw[:, lanes]) * cot[:, lanes].astype(F32)
        for e in range(2):
            part_lanes = slice(e * SIDE, (e + 1) * SIDE)
            at = 4 * b + 2 * e
            s_l[at : at + 2] = pair(val[:, part_lanes], up[:, part_lanes])
    for group in (1, 2):
        for slot in range(*GROUPS[group]):
            send(s_l.at[near(slot)], r1_l.at[BACK[slot]], "lq>", f">lq{group}", along_q(near(slot)))
    r1_l[0] = s_l[pl.ds(q, 1)].reshape(SIDE, SIDE)

    def onward(group):
        a, b = GROUPS[group]
        if group:
            arrived(r1_l.at[a:b], "lq>", f">lq{group}")
        for d in ORDER:
            peer = (z + d) % 8
            rows = pl.ds(pl.multiple_of(peer * 16, 16), 16)
            send(r1_l.at[a:b, rows, :], r2_l.at[z, a:b], "lz>", f">lz{group}", along_z(peer))
        mine = r1_l[a:b, pl.ds(pl.multiple_of(z * 16, 16), 16), :]
        r2_l[pl.ds(z, 1), a:b] = mine.reshape(1, b - a, 16, SIDE)

    def give(src, dst, at, who):
        send(src, dst, "tk>", f">tk{at}", who)

    up_half, down_half = slice(0, 64), slice(64, SIDE)
    ahead, behind = along_q(near(2)), along_q(near(3))
    beside, across = along_q(near(1)), (along_q(near(1))[0], opp)

    def sideways(block):
        give(tk.at[block, up_half], tk.at[block, up_half], 2, beside)
        give(tk.at[block, down_half], tk.at[block, down_half], 2, across)

    onward(0)
    for name in ("first", "twist", "second", "last"):
        loads[name].wait()
    cw = t_twist[0:64]
    sw = t_twist[64:128]
    for t in range(4):
        t_second16[t] = t_second[256 * t : 256 * (t + 1)].astype(BF16)
    t_first16[...] = t_first[...].astype(BF16)
    t_last16[...] = t_last[...].astype(BF16)
    g_high, g_low, i_high, i_low = (t_second16[t] for t in range(4))
    for b in range(4):
        lanes = slice(b * SIDE, (b + 1) * SIDE)
        s_c[2 * b : 2 * b + 2] = cot[:, lanes].astype(F32).T.astype(BF16).reshape(2, 64, SIDE)
    onward(1)
    onward(2)

    def regroup(src, dst):
        x = src[...].astype(F32).reshape(8, 8, 8, SIDE)
        for qq in range(8):
            dst[qq] = x[:, qq].reshape(64, SIDE).astype(BF16)

    arrived(r1_e.at[0:7], "ez>", ">ez")
    regroup(r1_e, s2_e)
    for d in ORDER:
        peer = (q + d) % 8
        send(s2_e.at[peer], r2_e.at[q], "eq>", ">eq", along_q(peer))
    r2_e[pl.ds(q, 1)] = s2_e[pl.ds(q, 1)]
    give(half, tk.at[q], 0, ahead)
    give(half, tk.at[q], 0, behind)
    give(tok.at[up_half, own_cols], tk.at[q, up_half], 0, beside)
    give(tok.at[down_half, own_cols], tk.at[q, down_half], 0, across)
    for d in ORDER:
        peer = (q + d) % 8
        send(s_c.at[peer], r_c.at[q], "cq>", ">cq", along_q(peer))
    r_c[pl.ds(q, 1)] = s_c[pl.ds(q, 1)]

    def put(at, x):
        high, low = halves(x)
        lhs[0, at * 64 : (at + 1) * 64] = high
        lhs[1, at * 64 : (at + 1) * 64] = low

    def forward(u, base, stride, out):
        for r in range(0, 8, 2):
            x = [u[pl.ds(base + r + e, 64, stride=stride), :] for e in range(2)]
            x = jnp.concatenate(x, axis=1).astype(BF16)
            a = dot(t_first16[...], jnp.concatenate([x, x], axis=0))
            for e in range(2):
                re = a[:64, e * SIDE : (e + 1) * SIDE]
                im = a[64:, e * SIDE : (e + 1) * SIDE]
                put(r + e, jnp.concatenate([re * cw + im * sw, im * cw - re * sw], axis=1))
        spec[out] = dot(lhs[0], g_high) + (dot(lhs[1], g_high) + dot(lhs[0], g_low))

    def inverse(left, right, conjugate, store):
        for r in range(8):
            rows = slice(r * 64, (r + 1) * 64)
            ar, ai = spec[left, rows, :SIDE], spec[left, rows, SIDE:]
            br, bi = spec[right, rows, :SIDE], spec[right, rows, SIDE:]
            if conjugate:
                p = [ar * br + ai * bi, ar * bi - ai * br]
            else:
                p = [ar * br - ai * bi, ar * bi + ai * br]
            put(r, jnp.concatenate(p, axis=1))
        mid[...] = dot(lhs[0], i_high) + (dot(lhs[1], i_high) + dot(lhs[0], i_low))
        for r in range(0, 8, 2):
            cols = []
            for e in range(2):
                rows = slice((r + e) * 64, (r + e + 1) * 64)
                re, im = mid[rows, :SIDE], mid[rows, SIDE:]
                cols.append(jnp.concatenate([re * cw - im * sw, im * cw + re * sw], axis=0))
            high, low = halves(jnp.concatenate(cols, axis=1))
            y = dot(t_last16[...], jnp.concatenate([high, low, high], axis=0))
            for e in range(2):
                store(r + e, y[:, e * SIDE : (e + 1) * SIDE])

    arrived(r2_e.at[0:7], "eq>", ">eq")
    for qq in range(8):
        x = r2_e[qq].astype(F32)
        for zz in range(8):
            u_e[zz * 64 + qq * 8 : zz * 64 + qq * 8 + 8] = x[zz * 8 : zz * 8 + 8]
    forward(u_e, 0, 8, 0)
    arrived(tk.at[0:3], "tk>", ">tk0")
    give(tk.at[near(2), up_half], tk.at[near(2), up_half], 1, behind)
    give(tk.at[near(3), down_half], tk.at[near(3), down_half], 1, ahead)
    sideways(near(2))
    sideways(near(3))
    for group, (a, b) in enumerate(GROUPS):
        arrived(r2_l.at[0:7, a:b], "lz>", f">lz{group}")
        for slot in range(a, b):
            for zz in range(8):
                at = pl.multiple_of(zz * SIDE + near(slot) * 16, 16)
                u_l[pl.ds(at, 16), :] = r2_l[zz, slot].astype(F32)
    forward(u_l, 8, 16, 2)
    forward(u_l, 0, 16, 1)

    def store_v(r, y):
        w_vg[pl.ds(r, 64, stride=16), :] = y

    def store_g(r, y):
        w_vg[pl.ds(8 + r, 64, stride=16), :] = y

    def store_f(r, y):
        w_f[pl.ds(r, 64, stride=8), :] = y

    inverse(0, 2, True, store_v)
    inverse(0, 1, False, store_g)
    for zz in range(8):
        s3[zz] = w_vg[zz * SIDE : (zz + 1) * SIDE].astype(BF16)
    for ds, mark in ((FAR, "f"), (CLOSE, "c")):
        for d in ds:
            peer = (z + d) % 8
            send(s3.at[peer], r3.at[z], "vz>", ">vz" + mark, along_z(peer))
    r3[pl.ds(z, 1)] = s3[pl.ds(z, 1)]
    inverse(1, 2, True, store_f)
    for zz in range(8):
        s3f[zz] = w_f[zz * 64 : (zz + 1) * 64].astype(BF16)
    arrived(tk.at[0], "tk>", ">tk1")
    sideways(near(6))

    arrived(r_c.at[0:7], "cq>", ">cq")
    wide_c[...] = r_c[...].astype(F32)

    def gate(at):
        x = r3[pl.ds(at, 1)].astype(F32).reshape(8, 16, SIDE)
        factor = wide_c[:, pl.ds(pl.multiple_of(at * 8, 8), 8), :]
        x = jnp.concatenate([x[:, :8], x[:, 8:] * factor], axis=1)
        r3[pl.ds(at, 1)] = x.astype(BF16).reshape(1, SIDE, SIDE)

    gate(z)
    send(r3.at[z], r3s.at[z], "sib>", ">sibc", (i, sib))
    for ds, mark in ((CLOSE, "c"), (FAR, "f")):
        arrived(r3.at[0 : len(ds)], "vz>", ">vz" + mark)
        for d in ds:
            peer = (z + d) % 8
            gate(peer)
            send(r3.at[peer], r3s.at[peer], "sib>", ">sib" + mark, (i, sib))
    for d in ORDER:
        peer = (q + d) % 8
        send(rows16(r3, peer), r4.at[q], "vq>", ">vq", along_q(peer))
    r4[pl.ds(q, 1)] = r3[:, pl.ds(pl.multiple_of(q * 16, 16), 16), :].reshape(1, 8, 16, SIDE)

    for d in ORDER:
        peer = (z + d) % 8
        send(s3f.at[peer], r3f.at[z], "fz>", ">fz", along_z(peer))
    r3f[pl.ds(z, 1)] = s3f[pl.ds(z, 1)]

    for qq in range(8):
        g_all[0:SIDE, qq * SIDE : (qq + 1) * SIDE] = r3[:, qq * 16 : (qq + 1) * 16, :].reshape(SIDE, SIDE)
    arrived(tk.at[0:3], "tk>", ">tk2")
    own.wait()
    arrived(r3s.at[0:5], "sib>", ">sibc")
    arrived(r3s.at[0:3], "sib>", ">sibf")
    for qq in range(8):
        g_all[SIDE:, qq * SIDE : (qq + 1) * SIDE] = r3s[:, qq * 16 : (qq + 1) * 16, :].reshape(SIDE, SIDE)
    for t in range(4):
        sums = dot(g_all[...], tk[:, :, t * 256 : (t + 1) * 256].reshape(1024, 256)).reshape(2, 8, 2, 8, 256)
        to = core * 4 + t
        for s, who in enumerate((c, sib)):
            rows = [sums[s, :, f].reshape(64, 256) for f in range(2)]
            at = (2 * t + s) * 8
            part[at : at + 8] = jnp.concatenate(rows, axis=0).T.astype(BF16).reshape(8, 32, SIDE)

            def share(slot, at=at, to=to, who=who):
                peer = near(slot)
                send(part.at[at + peer], r5.at[z * 8 + q], "rs>", ">rs", (to * 8 + peer, who))

            if s == 1:
                share(0)
            else:

                @pl.when(to != z)
                def _(share=share):
                    share(0)

                @pl.when(to == z)
                def _(at=at):
                    r5[pl.ds(z * 8 + q, 1)] = part[pl.ds(at + q, 1)]

            for slot in range(1, 8):
                share(slot)

    arrived(r4.at[0:7], "vq>", ">vq")
    for qq in range(8):
        x = r4[qq].astype(F32)
        vt[:, qq * 64 : (qq + 1) * 64] = x[:, :8].reshape(64, SIDE).T.astype(BF16)
        gt[:, qq * 64 : (qq + 1) * 64] = x[:, 8:].reshape(64, SIDE).T.astype(BF16)

    def columns(k):
        rows = pl.ds(pl.multiple_of(k * 512, 512), 512)
        over = (((1,), (1,)), ((), ()))
        a = lax.dot_general(vt[...], vw[rows, :], over, preferred_element_type=F32)
        return a + lax.dot_general(gt[...], gw[rows, :], over, preferred_element_type=F32)

    s7[0] = columns(2 * (1 - xh) + 1 - core)
    s7[1] = columns(2 * xh + 1 - core)
    send(s7, r7, "core>", ">core", (i, sib))
    far = columns(2 * (1 - xh) + core)
    here = columns(2 * xh + core)
    arrived(r7, "core>", ">core")
    s8[...] = (far + r7[0]).astype(BF16)
    send(s8, r8, "far>", ">far", (i, opp))
    here = here + r7[1]

    arrived(r3f.at[0:7], "fz>", ">fz")
    regroup(r3f, s4f)
    for d in ORDER:
        peer = (q + d) % 8
        send(s4f.at[peer], r4f.at[q], "fq>", ">fq", along_q(peer))
    r4f[pl.ds(q, 1)] = s4f[pl.ds(q, 1)]

    outs = [
        pltpu.make_async_copy(a, b, sem(f"out{t}"))
        for t, (a, b) in enumerate(zip((o_in, o_fil, o_vw, o_gw), (input_grad, filter_grad, vw_grad, gw_grad)))
    ]
    arrived(r8, "far>", ">far")
    o_in[...] = (here + r8[...].astype(F32)).astype(BF16)
    outs[0].start()
    arrived(r4f.at[0:7], "fq>", ">fq")
    for b in range(4):
        x = r4f[2 * b : 2 * b + 2].astype(F32).reshape(SIDE, SIDE)
        o_fil[:, b * SIDE : (b + 1) * SIDE] = x.T * SCALE
    outs[1].start()

    @pl.when(core == z // 4)
    def _():
        waiter(r5.at[0:63], "rs>", ">rs").wait()

    @pl.when(core != z // 4)
    def _():
        waiter(r5, "rs>", ">rs").wait()

    for qq in range(8):
        total = r5[qq].astype(F32)
        for zz in range(1, 8):
            total = total + r5[zz * 8 + qq].astype(F32)
        total = total * SCALE
        o_vw[:, qq * 64 : (qq + 1) * 64] = total[:, :64]
        o_gw[:, qq * 64 : (qq + 1) * 64] = total[:, 64:]
    outs[2].start()
    outs[3].start()

    for size, out in (
        (r1_e.at[0:7], "ez>"), (r2_e.at[0:7], "eq>"), (r1_l.at[0:7], "lq>"), (r2_l.at[0:7], "lz>"),
        (r3.at[0:7], "vz>"), (r_c.at[0:7], "cq>"), (r3s, "sib>"), (r3f.at[0:7], "fz>"), (r4.at[0:7], "vq>"), (r4f.at[0:7], "fq>"),
        (tk.at[0:7], "tk>"), (r7, "core>"), (r8, "far>"),
    ):
        waiter(size, out, ">ez").wait_send()
    for copy in outs:
        copy.wait()


def local(tokens, value_weight, gate_weight, filters, cotangent):
    def v(*shape, dtype=BF16):
        return pltpu.VMEM(shape, dtype)

    whole = pl.BlockSpec(memory_space=pl.ANY)
    operands = [tokens, value_weight, gate_weight, filters, cotangent]
    operands += [jnp.asarray(t) for t in tables()]
    shape = jax.ShapeDtypeStruct
    outputs = (shape((128, 512), BF16), shape((128, 512), F32), shape((32, 512), F32), shape((32, 512), F32))
    results = pl.pallas_call(
        kernel,
        out_shape=outputs,
        in_specs=[whole] * 9,
        out_specs=(whole,) * 4,
        scratch_shapes=[pltpu.VMEM(t.shape, t.dtype) for t in operands] + [
            v(128, 128), v(4, 256, 256), v(64, 384),
            v(8, 64, 128), v(8, 128, 128), v(8, 64, 128), v(8, 128, 128),
            v(8, 64, 128), v(8, 64, 128), v(8, 8, 16, 128),
            v(512, 128, dtype=F32), v(1024, 128, dtype=F32), v(1024, 128, dtype=F32), v(512, 128, dtype=F32),
            v(8, 64, 128), v(8, 64, 128), v(8, 64, 128, dtype=F32),
            v(3, 512, 256, dtype=F32), v(2, 512, 256), v(512, 256, dtype=F32),
            v(8, 128, 128), v(8, 128, 128), v(8, 128, 128), v(8, 8, 16, 128),
            v(8, 64, 128), v(8, 64, 128), v(8, 64, 128), v(8, 64, 128),
            v(8, 128, 1024), v(256, 1024), v(64, 32, 128), v(64, 32, 128),
            v(128, 512), v(128, 512),
            v(2, 128, 512, dtype=F32), v(2, 128, 512, dtype=F32), v(128, 512), v(128, 512),
        ] + [pltpu.VMEM(t.shape, t.dtype) for t in outputs] + [pltpu.SemaphoreType.DMA((len(SEMAPHORES),))],
        compiler_params=pltpu.CompilerParams(
            collective_id=0, has_side_effects=True, vmem_limit_bytes=60 * 1024 * 1024
        ),
        cost_estimate=pl.CostEstimate(flops=3_000_000_000, bytes_accessed=8_000_000, transcendentals=0),
    )(*operands)
    return pl.pallas_call(
        hand_over,
        out_shape=tuple(shape(r.shape, r.dtype) for r in results),
        in_specs=[whole] * 4,
        out_specs=(whole,) * 4,
        scratch_shapes=[pltpu.VMEM(r.shape, r.dtype) for r in results] + [pltpu.SemaphoreType.DMA((8,))],
        compiler_params=pltpu.CompilerParams(vmem_limit_bytes=60 * 1024 * 1024),
    )(*results)


def hand_over(*refs):
    into = [pltpu.make_async_copy(refs[t], refs[8 + t], refs[12].at[t]) for t in range(4)]
    onto = [pltpu.make_async_copy(refs[8 + t], refs[4 + t], refs[12].at[4 + t]) for t in range(4)]
    for copy in into:
        copy.start()
    for copy, after in zip(into, onto):
        copy.wait()
        after.start()
    for copy in onto:
        copy.wait()


def solution(mesh):
    placed = (P("seq", None), P(None, "ch"), P(None, "ch"), P("seq", "ch"), P("seq", "ch"))
    return jax.shard_map(
        local,
        mesh=mesh,
        in_specs=placed,
        out_specs=(P("seq", "ch"),) * 4,
        check_vma=False,
    )
```

time: 65.8 us -> 54.9 us (0.83)
  the two profiles are of different devices: /device:TPU:64 before, /device:TPU:1 now
where the time goes in v4:
time: 54.9 us; the launch traced here: 54.3 us
  Pallas kernels  53.7 us (98%)
  between operations  0.64 us (1%)
    pallas_call x1, Pallas kernels, local(): pl.pallas_call(kernel, out_shape=outputs, in_specs=[whole] * 9, out_specs...  51.8 us
    pallas_call x1, Pallas kernels, local(): pl.pallas_call(hand_over, out_shape=tuple((shape(r.shape, r.dtype) for r...  1.83 us

profile of v4, /device:TPU:1, one launch (start us, length us, event | category | flops | bytes accessed | tf_op | source)
XLA Modules:
  0.0 54.3 jit_solution(2345159347515996807)
XLA Ops:
  0.6 51.8 %shard_map.120 = (bf16[128,512]{1,0:T(8,128)(2,1)}, f32[128,512]{1,0:T(8,128)}, f32[32,512]{1,0:T(8,128)}, f32[32,512]{1,0:T(8,128)}) custom-call(bf16[128,2048]{1,0:T(8,128)(2,1)} %tok_in.1, bf16[2048,512]{1,0:T(8,128)(2,1)} %vw_in.1, bf16[2048,512]{1,0:T(8,128)(2,1)} %gw_in.1, f32[128,512]{1,0:T(8,128)} %fil_in.1, bf16[128,512]{1,0:T(8,128)(2,1)} %cot_in.1, ...), custom_call_target="tpu_custom_call" | custom-call | flops 3000000000 | bytes 8000000 | tf_op jit(solution)/shard_map/pallas_call | solution.py:454
  52.5 1.8 %shard_map.121 = (bf16[128,512]{1,0:T(8,128)(2,1)}, f32[128,512]{1,0:T(8,128)}, f32[32,512]{1,0:T(8,128)}, f32[32,512]{1,0:T(8,128)}) custom-call(bf16[128,512]{1,0:T(8,128)(2,1)} %get-tuple-element.8.refs_0_, f32[128,512]{1,0:T(8,128)} %get-tuple-element.9.refs_1_, f32[32,512]{1,0:T(8,128)} %get-tuple-element.10.refs_2_, f32[32,512]{1,0:T(8,128)} %get-tuple-element.11.refs_3_), custom_call_target="tpu_custom_call" | custom-call | tf_op jit(solution)/shard_map/pallas_call | solution.py:477

commit v5 on v4

--- a/solution.py
+++ b/solution.py
@@ -31,7 +31,7 @@
 SEMAPHORES = (
     tuple(t + ">" for t in OUTGOING)
     + tuple(">" + t for t in INCOMING)
-    + ("own", "out0", "out1", "out2", "out3")
+    + ("own", "self", "out0", "out1")
     + LOADS
 )
 
@@ -71,12 +71,12 @@
 
 def kernel(
     tok_in, vw_in, gw_in, fil_in, cot_in, t_first_in, t_twist_in, t_second_in, t_last_in,
-    input_grad, filter_grad, vw_grad, gw_grad,
+    input_grad, filter_grad, r5,
     tok, vw, gw, fil, cot, t_first, t_twist, t_second, t_last,
     t_first16, t_second16, t_last16, s_e, s_l, r1_e, r1_l, s2_e, r2_e, r2_l, u_e, u_l, w_vg, w_f,
     s_c, r_c, wide_c,
     spec, lhs, mid, s3, r3, r3s, r4, s3f, r3f, s4f, r4f,
-    tk, g_all, part, r5, vt, gt, s7, r7, s8, r8, o_in, o_fil, o_vw, o_gw, sems,
+    tk, g_all, part, vt, gt, s7, r7, s8, r8, o_in, o_fil, sems,
 ):
     i = lax.axis_index("seq")
     c = lax.axis_index("ch")
@@ -206,6 +206,10 @@
         lanes = slice(b * SIDE, (b + 1) * SIDE)
         s_c[2 * b : 2 * b + 2] = cot[:, lanes].astype(F32).T.astype(BF16).reshape(2, 64, SIDE)
     onward(1)
+    give(half, tk.at[q], 0, ahead)
+    give(half, tk.at[q], 0, behind)
+    give(tok.at[up_half, own_cols], tk.at[q, up_half], 0, beside)
+    give(tok.at[down_half, own_cols], tk.at[q, down_half], 0, across)
     onward(2)
 
     def regroup(src, dst):
@@ -219,10 +223,6 @@
         peer = (q + d) % 8
         send(s2_e.at[peer], r2_e.at[q], "eq>", ">eq", along_q(peer))
     r2_e[pl.ds(q, 1)] = s2_e[pl.ds(q, 1)]
-    give(half, tk.at[q], 0, ahead)
-    give(half, tk.at[q], 0, behind)
-    give(tok.at[up_half, own_cols], tk.at[q, up_half], 0, beside)
-    give(tok.at[down_half, own_cols], tk.at[q, down_half], 0, across)
     for d in ORDER:
         peer = (q + d) % 8
         send(s_c.at[peer], r_c.at[q], "cq>", ">cq", along_q(peer))
@@ -272,11 +272,6 @@
         for zz in range(8):
             u_e[zz * 64 + qq * 8 : zz * 64 + qq * 8 + 8] = x[zz * 8 : zz * 8 + 8]
     forward(u_e, 0, 8, 0)
-    arrived(tk.at[0:3], "tk>", ">tk0")
-    give(tk.at[near(2), up_half], tk.at[near(2), up_half], 1, behind)
-    give(tk.at[near(3), down_half], tk.at[near(3), down_half], 1, ahead)
-    sideways(near(2))
-    sideways(near(3))
     for group, (a, b) in enumerate(GROUPS):
         arrived(r2_l.at[0:7, a:b], "lz>", f">lz{group}")
         for slot in range(a, b):
@@ -304,6 +299,11 @@
             peer = (z + d) % 8
             send(s3.at[peer], r3.at[z], "vz>", ">vz" + mark, along_z(peer))
     r3[pl.ds(z, 1)] = s3[pl.ds(z, 1)]
+    arrived(tk.at[0:3], "tk>", ">tk0")
+    give(tk.at[near(2), up_half], tk.at[near(2), up_half], 1, behind)
+    give(tk.at[near(3), down_half], tk.at[near(3), down_half], 1, ahead)
+    sideways(near(2))
+    sideways(near(3))
     inverse(1, 2, True, store_f)
     for zz in range(8):
         s3f[zz] = w_f[zz * 64 : (zz + 1) * 64].astype(BF16)
@@ -367,7 +367,7 @@
 
                 @pl.when(to == z)
                 def _(at=at):
-                    r5[pl.ds(z * 8 + q, 1)] = part[pl.ds(at + q, 1)]
+                    pltpu.make_async_copy(part.at[at + q], r5.at[z * 8 + q], sem("self")).start()
 
             for slot in range(1, 8):
                 share(slot)
@@ -403,7 +403,7 @@
 
     outs = [
         pltpu.make_async_copy(a, b, sem(f"out{t}"))
-        for t, (a, b) in enumerate(zip((o_in, o_fil, o_vw, o_gw), (input_grad, filter_grad, vw_grad, gw_grad)))
+        for t, (a, b) in enumerate(zip((o_in, o_fil), (input_grad, filter_grad)))
     ]
     arrived(r8, "far>", ">far")
     o_in[...] = (here + r8[...].astype(F32)).astype(BF16)
@@ -417,20 +417,11 @@
     @pl.when(core == z // 4)
     def _():
         waiter(r5.at[0:63], "rs>", ">rs").wait()
+        pltpu.make_async_copy(part.at[0], r5.at[0], sem("self")).wait()
 
     @pl.when(core != z // 4)
     def _():
         waiter(r5, "rs>", ">rs").wait()
-
-    for qq in range(8):
-        total = r5[qq].astype(F32)
-        for zz in range(1, 8):
-            total = total + r5[zz * 8 + qq].astype(F32)
-        total = total * SCALE
-        o_vw[:, qq * 64 : (qq + 1) * 64] = total[:, :64]
-        o_gw[:, qq * 64 : (qq + 1) * 64] = total[:, 64:]
-    outs[2].start()
-    outs[3].start()
 
     for size, out in (
         (r1_e.at[0:7], "ez>"), (r2_e.at[0:7], "eq>"), (r1_l.at[0:7], "lq>"), (r2_l.at[0:7], "lz>"),
@@ -450,12 +441,13 @@
     operands = [tokens, value_weight, gate_weight, filters, cotangent]
     operands += [jnp.asarray(t) for t in tables()]
     shape = jax.ShapeDtypeStruct
-    outputs = (shape((128, 512), BF16), shape((128, 512), F32), shape((32, 512), F32), shape((32, 512), F32))
+    input_grad, filter_grad = shape((128, 512), BF16), shape((128, 512), F32)
+    weight_grad, terms = shape((32, 512), F32), shape((64, 32, 128), BF16)
     results = pl.pallas_call(
         kernel,
-        out_shape=outputs,
+        out_shape=(input_grad, filter_grad, terms),
         in_specs=[whole] * 9,
-        out_specs=(whole,) * 4,
+        out_specs=(whole,) * 3,
         scratch_shapes=[pltpu.VMEM(t.shape, t.dtype) for t in operands] + [
             v(128, 128), v(4, 256, 256), v(64, 384),
             v(8, 64, 128), v(8, 128, 128), v(8, 64, 128), v(8, 128, 128),
@@ -465,35 +457,55 @@
             v(3, 512, 256, dtype=F32), v(2, 512, 256), v(512, 256, dtype=F32),
             v(8, 128, 128), v(8, 128, 128), v(8, 128, 128), v(8, 8, 16, 128),
             v(8, 64, 128), v(8, 64, 128), v(8, 64, 128), v(8, 64, 128),
-            v(8, 128, 1024), v(256, 1024), v(64, 32, 128), v(64, 32, 128),
+            v(8, 128, 1024), v(256, 1024), v(64, 32, 128),
             v(128, 512), v(128, 512),
             v(2, 128, 512, dtype=F32), v(2, 128, 512, dtype=F32), v(128, 512), v(128, 512),
-        ] + [pltpu.VMEM(t.shape, t.dtype) for t in outputs] + [pltpu.SemaphoreType.DMA((len(SEMAPHORES),))],
+        ] + [pltpu.VMEM(t.shape, t.dtype) for t in (input_grad, filter_grad)] + [pltpu.SemaphoreType.DMA((len(SEMAPHORES),))],
         compiler_params=pltpu.CompilerParams(
             collective_id=0, has_side_effects=True, vmem_limit_bytes=60 * 1024 * 1024
         ),
         cost_estimate=pl.CostEstimate(flops=3_000_000_000, bytes_accessed=8_000_000, transcendentals=0),
     )(*operands)
+    outputs = (input_grad, filter_grad, weight_grad, weight_grad)
     return pl.pallas_call(
-        hand_over,
-        out_shape=tuple(shape(r.shape, r.dtype) for r in results),
-        in_specs=[whole] * 4,
+        finish,
+        out_shape=outputs,
+        in_specs=[whole] * 3,
         out_specs=(whole,) * 4,
-        scratch_shapes=[pltpu.VMEM(r.shape, r.dtype) for r in results] + [pltpu.SemaphoreType.DMA((8,))],
+        scratch_shapes=[pltpu.VMEM(t.shape, t.dtype) for t in outputs + (terms,)] + [pltpu.SemaphoreType.DMA((7,))],
         compiler_params=pltpu.CompilerParams(vmem_limit_bytes=60 * 1024 * 1024),
     )(*results)
 
 
-def hand_over(*refs):
-    into = [pltpu.make_async_copy(refs[t], refs[8 + t], refs[12].at[t]) for t in range(4)]
-    onto = [pltpu.make_async_copy(refs[8 + t], refs[4 + t], refs[12].at[4 + t]) for t in range(4)]
-    for copy in into:
-        copy.start()
-    for copy, after in zip(into, onto):
-        copy.wait()
-        after.start()
-    for copy in onto:
-        copy.wait()
+def finish(
+    in_grad_in, filter_grad_in, terms_in, in_grad, filter_grad, vw_grad, gw_grad,
+    o_in, o_fil, o_vw, o_gw, terms, sems,
+):
+    loads = [
+        pltpu.make_async_copy(a, b, sems.at[t])
+        for t, (a, b) in enumerate(((terms_in, terms), (in_grad_in, o_in), (filter_grad_in, o_fil)))
+    ]
+    for load in loads:
+        load.start()
+    stores = [
+        pltpu.make_async_copy(a, b, sems.at[3 + t])
+        for t, (a, b) in enumerate(((o_in, in_grad), (o_fil, filter_grad), (o_vw, vw_grad), (o_gw, gw_grad)))
+    ]
+    loads[0].wait()
+    for qq in range(8):
+        total = terms[qq].astype(F32)
+        for zz in range(1, 8):
+            total = total + terms[zz * 8 + qq].astype(F32)
+        total = total * SCALE
+        o_vw[:, qq * 64 : (qq + 1) * 64] = total[:, :64]
+        o_gw[:, qq * 64 : (qq + 1) * 64] = total[:, 64:]
+    stores[2].start()
+    stores[3].start()
+    for t in (1, 2):
+        loads[t].wait()
+        stores[t - 1].start()
+    for store in stores:
+        store.wait()
 
 
 def solution(mesh):

time: 54.9 us -> 56.4 us (1.027)
  Pallas kernels: 53.7 us -> 55.6 us
    pallas_call x2, Pallas kernels: 53.7 us -> 55.6 us  [the longest x1 53.6 us: local(): pl.pallas_call(kernel, out_shape=(input_grad, filter_grad, terms), in_spe...]
where the time goes in v5:
time: 56.4 us; the launch traced here: 56.3 us
  Pallas kernels  55.6 us (99%)
  between operations  0.64 us (1%)
    pallas_call x1, Pallas kernels, local(): pl.pallas_call(kernel, out_shape=(input_grad, filter_grad, terms), in_spe...  53.6 us
    pallas_call x1, Pallas kernels, local(): pl.pallas_call(finish, out_shape=outputs, in_specs=[whole] * 3, out_specs...  2.04 us

profile of v5, /device:TPU:1, one launch (start us, length us, event | category | flops | bytes accessed | tf_op | source)
XLA Modules:
  0.0 56.3 jit_solution(2767692893510720927)
XLA Ops:
  0.6 53.6 %shard_map.120 = (bf16[128,512]{1,0:T(8,128)(2,1)}, f32[128,512]{1,0:T(8,128)}, bf16[64,32,128]{2,1,0:T(8,128)(2,1)}) custom-call(bf16[128,2048]{1,0:T(8,128)(2,1)} %tok_in.1, bf16[2048,512]{1,0:T(8,128)(2,1)} %vw_in.1, bf16[2048,512]{1,0:T(8,128)(2,1)} %gw_in.1, f32[128,512]{1,0:T(8,128)} %fil_in.1, bf16[128,512]{1,0:T(8,128)(2,1)} %cot_in.1, ...), custom_call_target="tpu_custom_call" | custom-call | flops 3000000000 | bytes 8000000 | tf_op jit(solution)/shard_map/pallas_call | solution.py:446
  54.2 2.0 %shard_map.121 = (bf16[128,512]{1,0:T(8,128)(2,1)}, f32[128,512]{1,0:T(8,128)}, f32[32,512]{1,0:T(8,128)}, f32[32,512]{1,0:T(8,128)}) custom-call(bf16[128,512]{1,0:T(8,128)(2,1)} %get-tuple-element.7.in_grad_in, f32[128,512]{1,0:T(8,128)} %get-tuple-element.8.filter_grad_in, bf16[64,32,128]{2,1,0:T(8,128)(2,1)} %get-tuple-element.9.terms_in), custom_call_target="tpu_custom_call" | custom-call | tf_op jit(solution)/shard_map/pallas_call | solution.py:470

commit v6 on v5

--- a/solution.py
+++ b/solution.py
@@ -148,12 +148,30 @@
     own = pltpu.make_async_copy(half, tk.at[q], sem("own"))
     own.start()
 
+    def give(src, dst, at, who):
+        send(src, dst, "tk>", f">tk{at}", who)
+
+    up_half, down_half = slice(0, 64), slice(64, SIDE)
+    ahead, behind = along_q(near(2)), along_q(near(3))
+    beside, across = along_q(near(1)), (along_q(near(1))[0], opp)
+
+    def sideways(block):
+        give(tk.at[block, up_half], tk.at[block, up_half], 2, beside)
+        give(tk.at[block, down_half], tk.at[block, down_half], 2, across)
+
+    def pieces(first, last):
+        for k in range(first, last):
+            rows = slice(16 * k, 16 * (k + 1))
+            for who in (ahead, behind, beside if k < 4 else across):
+                give(tok.at[rows, own_cols], tk.at[q, rows], 0, who)
+
     pl.semaphore_wait(barrier, peers)
     for d in ORDER:
         peer = (z + d) % 8
         send(s_e.at[peer], r1_e.at[z], "ez>", ">ez", along_z(peer))
     r1_e[pl.ds(z, 1)] = s_e[pl.ds(z, 1)]
 
+    pieces(0, 2)
     loads["cot"].wait()
     loads["vw"].wait()
     loads["gw"].wait()
@@ -170,6 +188,7 @@
             send(s_l.at[near(slot)], r1_l.at[BACK[slot]], "lq>", f">lq{group}", along_q(near(slot)))
     r1_l[0] = s_l[pl.ds(q, 1)].reshape(SIDE, SIDE)
 
+    pieces(2, 4)
     def onward(group):
         a, b = GROUPS[group]
         if group:
@@ -180,17 +199,6 @@
             send(r1_l.at[a:b, rows, :], r2_l.at[z, a:b], "lz>", f">lz{group}", along_z(peer))
         mine = r1_l[a:b, pl.ds(pl.multiple_of(z * 16, 16), 16), :]
         r2_l[pl.ds(z, 1), a:b] = mine.reshape(1, b - a, 16, SIDE)
-
-    def give(src, dst, at, who):
-        send(src, dst, "tk>", f">tk{at}", who)
-
-    up_half, down_half = slice(0, 64), slice(64, SIDE)
-    ahead, behind = along_q(near(2)), along_q(near(3))
-    beside, across = along_q(near(1)), (along_q(near(1))[0], opp)
-
-    def sideways(block):
-        give(tk.at[block, up_half], tk.at[block, up_half], 2, beside)
-        give(tk.at[block, down_half], tk.at[block, down_half], 2, across)
 
     onward(0)
     for name in ("first", "twist", "second", "last"):
@@ -206,12 +214,10 @@
         lanes = slice(b * SIDE, (b + 1) * SIDE)
         s_c[2 * b : 2 * b + 2] = cot[:, lanes].astype(F32).T.astype(BF16).reshape(2, 64, SIDE)
     onward(1)
-    give(half, tk.at[q], 0, ahead)
-    give(half, tk.at[q], 0, behind)
-    give(tok.at[up_half, own_cols], tk.at[q, up_half], 0, beside)
-    give(tok.at[down_half, own_cols], tk.at[q, down_half], 0, across)
+    pieces(4, 5)
     onward(2)
 
+    pieces(5, 6)
     def regroup(src, dst):
         x = src[...].astype(F32).reshape(8, 8, 8, SIDE)
         for qq in range(8):
@@ -223,6 +229,7 @@
         peer = (q + d) % 8
         send(s2_e.at[peer], r2_e.at[q], "eq>", ">eq", along_q(peer))
     r2_e[pl.ds(q, 1)] = s2_e[pl.ds(q, 1)]
+    pieces(6, 8)
     for d in ORDER:
         peer = (q + d) % 8
         send(s_c.at[peer], r_c.at[q], "cq>", ">cq", along_q(peer))
@@ -278,6 +285,11 @@
             for zz in range(8):
                 at = pl.multiple_of(zz * SIDE + near(slot) * 16, 16)
                 u_l[pl.ds(at, 16), :] = r2_l[zz, slot].astype(F32)
+    arrived(tk.at[0:3], "tk>", ">tk0")
+    give(tk.at[near(2), up_half], tk.at[near(2), up_half], 1, behind)
+    give(tk.at[near(3), down_half], tk.at[near(3), down_half], 1, ahead)
+    sideways(near(2))
+    sideways(near(3))
     forward(u_l, 8, 16, 2)
     forward(u_l, 0, 16, 1)
 
@@ -299,17 +311,12 @@
             peer = (z + d) % 8
             send(s3.at[peer], r3.at[z], "vz>", ">vz" + mark, along_z(peer))
     r3[pl.ds(z, 1)] = s3[pl.ds(z, 1)]
-    arrived(tk.at[0:3], "tk>", ">tk0")
-    give(tk.at[near(2), up_half], tk.at[near(2), up_half], 1, behind)
-    give(tk.at[near(3), down_half], tk.at[near(3), down_half], 1, ahead)
-    sideways(near(2))
-    sideways(near(3))
     inverse(1, 2, True, store_f)
     for zz in range(8):
         s3f[zz] = w_f[zz * 64 : (zz + 1) * 64].astype(BF16)
+
     arrived(tk.at[0], "tk>", ">tk1")
     sideways(near(6))
-
     arrived(r_c.at[0:7], "cq>", ">cq")
     wide_c[...] = r_c[...].astype(F32)
 

time: 56.4 us -> 52.9 us (0.938)
  Pallas kernels: 55.6 us -> 52.2 us
    pallas_call x1, Pallas kernels: 53.6 us -> 50.1 us  [local(): pl.pallas_call(kernel, out_shape=(input_grad, filter_grad, terms), in_spe...]
where the time goes in v6:
time: 52.9 us; the launch traced here: 52.8 us
  Pallas kernels  52.2 us (99%)
  between operations  0.64 us (1%)
    pallas_call x1, Pallas kernels, local(): pl.pallas_call(kernel, out_shape=(input_grad, filter_grad, terms), in_spe...  50.1 us
    pallas_call x1, Pallas kernels, local(): pl.pallas_call(finish, out_shape=outputs, in_specs=[whole] * 3, out_specs...  2.04 us

profile of v6, /device:TPU:1, one launch (start us, length us, event | category | flops | bytes accessed | tf_op | source)
XLA Modules:
  0.0 52.8 jit_solution(1462895363516177599)
XLA Ops:
  0.6 50.1 %shard_map.120 = (bf16[128,512]{1,0:T(8,128)(2,1)}, f32[128,512]{1,0:T(8,128)}, bf16[64,32,128]{2,1,0:T(8,128)(2,1)}) custom-call(bf16[128,2048]{1,0:T(8,128)(2,1)} %tok_in.1, bf16[2048,512]{1,0:T(8,128)(2,1)} %vw_in.1, bf16[2048,512]{1,0:T(8,128)(2,1)} %gw_in.1, f32[128,512]{1,0:T(8,128)} %fil_in.1, bf16[128,512]{1,0:T(8,128)(2,1)} %cot_in.1, ...), custom_call_target="tpu_custom_call" | custom-call | flops 3000000000 | bytes 8000000 | tf_op jit(solution)/shard_map/pallas_call | solution.py:453
  50.8 2.0 %shard_map.121 = (bf16[128,512]{1,0:T(8,128)(2,1)}, f32[128,512]{1,0:T(8,128)}, f32[32,512]{1,0:T(8,128)}, f32[32,512]{1,0:T(8,128)}) custom-call(bf16[128,512]{1,0:T(8,128)(2,1)} %get-tuple-element.7.in_grad_in, f32[128,512]{1,0:T(8,128)} %get-tuple-element.8.filter_grad_in, bf16[64,32,128]{2,1,0:T(8,128)(2,1)} %get-tuple-element.9.terms_in), custom_call_target="tpu_custom_call" | custom-call | tf_op jit(solution)/shard_map/pallas_call | solution.py:477

commit v7 on v6

--- a/solution.py
+++ b/solution.py
@@ -215,9 +215,6 @@
         s_c[2 * b : 2 * b + 2] = cot[:, lanes].astype(F32).T.astype(BF16).reshape(2, 64, SIDE)
     onward(1)
     pieces(4, 5)
-    onward(2)
-
-    pieces(5, 6)
     def regroup(src, dst):
         x = src[...].astype(F32).reshape(8, 8, 8, SIDE)
         for qq in range(8):
@@ -229,6 +226,9 @@
         peer = (q + d) % 8
         send(s2_e.at[peer], r2_e.at[q], "eq>", ">eq", along_q(peer))
     r2_e[pl.ds(q, 1)] = s2_e[pl.ds(q, 1)]
+    onward(2)
+
+    pieces(5, 6)
     pieces(6, 8)
     for d in ORDER:
         peer = (q + d) % 8

time: 52.9 us -> 52.6 us (level); the launches traced: 52.8 us -> 51.9 us
  Pallas kernels: 52.2 us -> 51.3 us
    pallas_call x1, Pallas kernels: 50.1 us -> 49.3 us  [local(): pl.pallas_call(kernel, out_shape=(input_grad, filter_grad, terms), in_spe...]
where the time goes in v7:
time: 52.6 us; the launch traced here: 51.9 us
  Pallas kernels  51.3 us (98%)
  between operations  0.64 us (1%)
    pallas_call x1, Pallas kernels, local(): pl.pallas_call(kernel, out_shape=(input_grad, filter_grad, terms), in_spe...  49.3 us
    pallas_call x1, Pallas kernels, local(): pl.pallas_call(finish, out_shape=outputs, in_specs=[whole] * 3, out_specs...  2.04 us

profile of v7, /device:TPU:1, one launch (start us, length us, event | category | flops | bytes accessed | tf_op | source)
XLA Modules:
  0.0 51.9 jit_solution(1572345042998745627)
XLA Ops:
  0.6 49.3 %shard_map.120 = (bf16[128,512]{1,0:T(8,128)(2,1)}, f32[128,512]{1,0:T(8,128)}, bf16[64,32,128]{2,1,0:T(8,128)(2,1)}) custom-call(bf16[128,2048]{1,0:T(8,128)(2,1)} %tok_in.1, bf16[2048,512]{1,0:T(8,128)(2,1)} %vw_in.1, bf16[2048,512]{1,0:T(8,128)(2,1)} %gw_in.1, f32[128,512]{1,0:T(8,128)} %fil_in.1, bf16[128,512]{1,0:T(8,128)(2,1)} %cot_in.1, ...), custom_call_target="tpu_custom_call" | custom-call | flops 3000000000 | bytes 8000000 | tf_op jit(solution)/shard_map/pallas_call | solution.py:453
  49.9 2.0 %shard_map.121 = (bf16[128,512]{1,0:T(8,128)(2,1)}, f32[128,512]{1,0:T(8,128)}, f32[32,512]{1,0:T(8,128)}, f32[32,512]{1,0:T(8,128)}) custom-call(bf16[128,512]{1,0:T(8,128)(2,1)} %get-tuple-element.7.in_grad_in, f32[128,512]{1,0:T(8,128)} %get-tuple-element.8.filter_grad_in, bf16[64,32,128]{2,1,0:T(8,128)(2,1)} %get-tuple-element.9.terms_in), custom_call_target="tpu_custom_call" | custom-call | tf_op jit(solution)/shard_map/pallas_call | solution.py:477

commit v8 on v7

--- a/solution.py
+++ b/solution.py
@@ -171,7 +171,7 @@
         send(s_e.at[peer], r1_e.at[z], "ez>", ">ez", along_z(peer))
     r1_e[pl.ds(z, 1)] = s_e[pl.ds(z, 1)]
 
-    pieces(0, 2)
+    pieces(0, 3)
     loads["cot"].wait()
     loads["vw"].wait()
     loads["gw"].wait()
@@ -188,7 +188,7 @@
             send(s_l.at[near(slot)], r1_l.at[BACK[slot]], "lq>", f">lq{group}", along_q(near(slot)))
     r1_l[0] = s_l[pl.ds(q, 1)].reshape(SIDE, SIDE)
 
-    pieces(2, 4)
+    pieces(3, 5)
     def onward(group):
         a, b = GROUPS[group]
         if group:
@@ -214,7 +214,7 @@
         lanes = slice(b * SIDE, (b + 1) * SIDE)
         s_c[2 * b : 2 * b + 2] = cot[:, lanes].astype(F32).T.astype(BF16).reshape(2, 64, SIDE)
     onward(1)
-    pieces(4, 5)
+    pieces(5, 6)
     def regroup(src, dst):
         x = src[...].astype(F32).reshape(8, 8, 8, SIDE)
         for qq in range(8):
@@ -228,8 +228,8 @@
     r2_e[pl.ds(q, 1)] = s2_e[pl.ds(q, 1)]
     onward(2)
 
-    pieces(5, 6)
-    pieces(6, 8)
+    pieces(6, 7)
+    pieces(7, 8)
     for d in ORDER:
         peer = (q + d) % 8
         send(s_c.at[peer], r_c.at[q], "cq>", ">cq", along_q(peer))

time: 52.6 us -> 53.4 us (1.015); the launches traced: 51.9 us -> 53.3 us
  Pallas kernels: 51.3 us -> 52.6 us
    pallas_call x1, Pallas kernels: 49.3 us -> 50.6 us  [local(): pl.pallas_call(kernel, out_shape=(input_grad, filter_grad, terms), in_spe...]
where the time goes in v8:
time: 53.4 us; the launch traced here: 53.3 us
  Pallas kernels  52.6 us (99%)
  between operations  0.64 us (1%)
    pallas_call x1, Pallas kernels, local(): pl.pallas_call(kernel, out_shape=(input_grad, filter_grad, terms), in_spe...  50.6 us
    pallas_call x1, Pallas kernels, local(): pl.pallas_call(finish, out_shape=outputs, in_specs=[whole] * 3, out_specs...  2.04 us

profile of v8, /device:TPU:1, one launch (start us, length us, event | category | flops | bytes accessed | tf_op | source)
XLA Modules:
  0.0 53.3 jit_solution(14079380414529182328)
XLA Ops:
  0.6 50.6 %shard_map.120 = (bf16[128,512]{1,0:T(8,128)(2,1)}, f32[128,512]{1,0:T(8,128)}, bf16[64,32,128]{2,1,0:T(8,128)(2,1)}) custom-call(bf16[128,2048]{1,0:T(8,128)(2,1)} %tok_in.1, bf16[2048,512]{1,0:T(8,128)(2,1)} %vw_in.1, bf16[2048,512]{1,0:T(8,128)(2,1)} %gw_in.1, f32[128,512]{1,0:T(8,128)} %fil_in.1, bf16[128,512]{1,0:T(8,128)(2,1)} %cot_in.1, ...), custom_call_target="tpu_custom_call" | custom-call | flops 3000000000 | bytes 8000000 | tf_op jit(solution)/shard_map/pallas_call | solution.py:453
  51.2 2.0 %shard_map.121 = (bf16[128,512]{1,0:T(8,128)(2,1)}, f32[128,512]{1,0:T(8,128)}, f32[32,512]{1,0:T(8,128)}, f32[32,512]{1,0:T(8,128)}) custom-call(bf16[128,512]{1,0:T(8,128)(2,1)} %get-tuple-element.7.in_grad_in, f32[128,512]{1,0:T(8,128)} %get-tuple-element.8.filter_grad_in, bf16[64,32,128]{2,1,0:T(8,128)(2,1)} %get-tuple-element.9.terms_in), custom_call_target="tpu_custom_call" | custom-call | tf_op jit(solution)/shard_map/pallas_call | solution.py:477
